TPU v7x, 32 devices: a whole 2x2x4 slice. The times are simulated.
32 devices in a mesh: row: 8 (over z, core), col: 4 (over y, x).
Axes of the slice: x: 2, y: 2, z: 4, core: 2. Of those that a mesh axis runs over, the one named last changes fastest.
Arguments:
- rhs_top: bfloat16 [2, 1024, 4096], P(None, 'row', 'col'), may hold values from -6 to 6
- diag_inverse: bfloat16 [2, 1024, 1024], P(None, 'row'), as said below
- panel_coupling: bfloat16 [1024, 1024], P('row'), may hold values from -0.1875 to 0.1875
- trailing_factor: bfloat16 [8192, 2048], P('row', 'col'), may hold values from -0.125 to 0.125
- rhs_trailing: bfloat16 [8192, 4096], P('row', 'col'), may hold values from -6 to 6
Outputs:
- solved: bfloat16 [2, 1024, 4096], P(None, 'row', 'col')
- updated: bfloat16 [8192, 4096], P('row', 'col')
Inputs may be any that keep to these rules, and one draw needn't show every extreme that they name: Each diag_inverse[k] is lower triangular.
All inputs are finite; a program needn't handle non-finite values.
Results may differ from a plain program's by a relative error of at most 0.0055.
Values may be sent and summed in bfloat16 or wider, within the bound.
No kernel may reach another device: no remote copies, remote signals or barrier semaphores. Data moves between devices by JAX's collectives and lax.ppermute only.
A program may use at most 64 MiB of HBM per device.

v0:
```python
import jax
import jax.numpy as jnp
from jax import lax
from jax.sharding import PartitionSpec as P


def fold_rows(inverse_rows, piece):
    return jnp.dot(inverse_rows, piece, preferred_element_type=jnp.float32)


def shards(rhs_top, diag_inverse, panel_coupling, trailing_factor, rhs_trailing):
    inverse_first = diag_inverse[0]
    inverse_second = diag_inverse[1]
    first_mine = fold_rows(
        inverse_first, lax.all_gather(rhs_top[0], "row", axis=0, tiled=True)
    ).astype(jnp.bfloat16)
    first_all = lax.all_gather(first_mine, "row", axis=0, tiled=True)
    carried = (
        rhs_top[1].astype(jnp.float32)
        - jnp.dot(panel_coupling, first_all, preferred_element_type=jnp.float32)
    ).astype(jnp.bfloat16)
    second_mine = fold_rows(
        inverse_second, lax.all_gather(carried, "row", axis=0, tiled=True)
    ).astype(jnp.bfloat16)
    second_all = lax.all_gather(second_mine, "row", axis=0, tiled=True)
    solution = jnp.concatenate([first_all, second_all], axis=0)
    total = jnp.dot(
        lax.all_gather(trailing_factor, "col", axis=1, tiled=True),
        solution,
        preferred_element_type=jnp.float32,
    )
    updated = (rhs_trailing.astype(jnp.float32) - total).astype(jnp.bfloat16)
    solved = jnp.stack([first_mine, second_mine])
    return (solved, updated)


def solution(mesh):
    in_specs = (
        P(None, "row", "col"),
        P(None, "row", None),
        P("row", None),
        P("row", "col"),
        P("row", "col"),
    )
    out_specs = (P(None, "row", "col"), P("row", "col"))
    return jax.shard_map(shards, mesh=mesh, in_specs=in_specs, out_specs=out_specs, check_vma=False)
```

profile of v0, /device:TPU:0, one launch (start us, length us, event | category | flops | bytes accessed | tf_op | source)
XLA Modules:
  0.0 207.2 jit_solution(3586734224011820467)
XLA Ops:
  7.2 0.0 copy-start
  7.2 0.0 copy-start.5
  7.2 0.0 all-gather.15.cloned.1.call-start
  7.2 1.7 slice.13
  9.0 0.0 all-gather.15.cloned.1.call-update
  9.0 0.0 all-gather.7.cloned.1.call-start
  9.0 33.0 %all-gather.15.cloned.1.call-done = bf16[1,1024,1024]{2,1,0:T(8,128)(2,1)} async-done(((bf16[1,128,1024]{2,1,0:T(8,128)(2,1)}), bf16[1,1024,1024]{2,1,0:T(8,128)(2,1)}) %all-gather.15.cloned.1.call-update) | async-done | bytes 2097168 | tf_op jit(solution)/shard_map/all_gather | solution.py:15
  42.0 2.8 %fusion.10 = bf16[128,1024]{1,0:T(8,128)(2,1)} fusion(bf16[1,1024,1024]{2,1,0:T(8,128)(2,1)} %all-gather.15.cloned.1.call-done, bf16[2,128,1024]{2,1,0:T(8,128)(2,1)} %param.6), kind=kOutput, calls=%fused_computation.10 | convolution fusion | flops 268566528 | bytes 2621440 | tf_op jit(solution)/shard_map/dot_general | solution.py:8
  44.9 0.0 all-gather.7.cloned.1.call-update
  44.9 0.0 copy-start.4
  44.9 0.0 all-gather.9.cloned.1.call-start
  45.0 28.7 %all-gather.7.cloned.1.call-done = bf16[1024,1024]{1,0:T(8,128)(2,1)} async-done(((bf16[128,1024]{1,0:T(8,128)(2,1)}), bf16[1024,1024]{1,0:T(8,128)(2,1)}) %all-gather.7.cloned.1.call-update) | async-done | bytes 2097168 | tf_op jit(solution)/shard_map/all_gather | solution.py:17
  73.6 0.0 copy-done
  73.7 0.0 copy-done.5
  73.7 2.7 %fusion.13 = bf16[128,1024]{1,0:T(8,128)(2,1)} fusion(bf16[128,1024]{1,0:T(8,128)(2,1)S(1)} %copy-done, bf16[1024,1024]{1,0:T(8,128)(2,1)} %all-gather.7.cloned.1.call-done, bf16[2,128,1024]{2,1,0:T(8,128)(2,1)S(1)} %copy-done.5), kind=kOutput, calls=%fused_computation.12 | convolution fusion | flops 268828672 | bytes 2883584 | tf_op jit(solution)/shard_map/dot_general | solution.py:20
  76.4 0.0 copy-start.3
  76.4 0.0 all-gather.9.cloned.1.call-update
  76.4 0.0 all-gather.13.cloned.1.call-start
  76.5 0.5 all-gather.13.cloned.1.call-update
  77.0 0.0 all-gather.11.cloned.1.call-start
  77.0 28.1 %all-gather.9.cloned.1.call-done = bf16[1024,1024]{1,0:T(8,128)(2,1)} async-done(((bf16[128,1024]{1,0:T(8,128)(2,1)}), bf16[1024,1024]{1,0:T(8,128)(2,1)}) %all-gather.9.cloned.1.call-update) | async-done | bytes 2097168 | tf_op jit(solution)/shard_map/all_gather | solution.py:23
  105.2 0.0 copy-done.4
  105.2 2.7 %convolution_convert_fusion = bf16[1024,128]{0,1:T(8,128)(2,1)} fusion(bf16[1024,1024]{1,0:T(8,128)(2,1)} %all-gather.9.cloned.1.call-done, bf16[2,128,1024]{2,1,0:T(8,128)(2,1)S(1)} %copy-done.4), kind=kOutput, calls=%fused_computation.11 | convolution fusion | flops 268566528 | bytes 2621440 | tf_op jit(solution)/shard_map/dot_general | solution.py:8
  107.9 0.0 all-gather.11.cloned.1.call-update
  108.0 0.0 copy-done.3
  108.0 0.0 copy-start.1
  108.0 0.0 copy-start.2
  108.0 2.6 %copy.8 = bf16[1024,1024]{0,1:T(8,128)(2,1)} copy(bf16[1024,1024]{1,0:T(8,128)(2,1)S(1)} %copy-done.3) | data formatting | bytes 4194304 | tf_op args[4]
  110.5 0.0 copy-done.1
  110.5 0.0 copy-done.2
  110.5 0.8 pad_maximum_fusion
  111.4 47.6 %all-gather.13.cloned.1.call-done = bf16[1024,2048]{1,0:T(8,128)(2,1)} async-done(((bf16[1024,512]{1,0:T(8,128)(2,1)}), bf16[1024,2048]{1,0:T(8,128)(2,1)}) %all-gather.13.cloned.1.call-update) | async-done | bytes 4194320 | tf_op jit(solution)/shard_map/all_gather | solution.py:28
  158.9 30.6 %all-gather.11.cloned.1.call-done = bf16[1024,1024]{1,0:T(8,128)(2,1)} async-done(((bf16[128,1024]{1,0:T(8,128)(2,1)}), bf16[1024,1024]{1,0:T(8,128)(2,1)}) %all-gather.11.cloned.1.call-update) | async-done | bytes 2097168 | tf_op jit(solution)/shard_map/all_gather | solution.py:25
  189.5 8.6 %fusion.4 = bf16[1024,1024]{0,1:T(8,128)(2,1)S(1)} fusion(bf16[1024,1024]{0,1:T(8,128)(2,1)} %copy.8, bf16[1024,2048]{1,0:T(8,128)(2,1)} %all-gather.13.cloned.1.call-done, bf16[1024,1024]{1,0:T(8,128)(2,1)} %all-gather.11.cloned.1.call-done, bf16[1024,1024]{1,0:T(8,128)(2,1)} %all-gather.7.cloned.1.call-done), kind=kOutput, calls=%fused_computation.5 | convolution fusion | flops 4306501632 | bytes 12582912 | tf_op jit(solution)/shard_map/dot_general | solution.py:27
  198.1 2.6 %copy.9 = bf16[1024,1024]{1,0:T(8,128)(2,1)} copy(bf16[1024,1024]{0,1:T(8,128)(2,1)S(1)} %fusion.4) | data formatting | bytes 4194304
Async XLA Ops:
  7.2 66.5 %copy-start = (bf16[128,1024]{1,0:T(8,128)(2,1)S(1)}, bf16[128,1024]{1,0:T(8,128)(2,1)}, u32[]{:S(2)}) copy-start(bf16[128,1024]{1,0:T(8,128)(2,1)} %param.7) | copy-start | bytes 786436
  7.2 66.5 %copy-start.5 = (bf16[2,128,1024]{2,1,0:T(8,128)(2,1)S(1)}, bf16[2,128,1024]{2,1,0:T(8,128)(2,1)}, u32[]{:S(2)}) copy-start(bf16[2,128,1024]{2,1,0:T(8,128)(2,1)} %param.5) | copy-start | bytes 1572868
  7.2 34.8 %all-gather.15.cloned.1.call-start = ((), (), s32[]{:S(2)}) async-start(), calls=%async_computation.4 | async-start | bytes 2359296 | tf_op jit(solution)/shard_map/all_gather | solution.py:15
  9.0 64.7 %all-gather.7.cloned.1.call-start = ((), (), s32[]{:S(2)}) async-start(), calls=%async_computation | async-start | bytes 2359296 | tf_op jit(solution)/shard_map/all_gather | solution.py:17
  44.9 60.3 %copy-start.4 = (bf16[2,128,1024]{2,1,0:T(8,128)(2,1)S(1)}, bf16[2,128,1024]{2,1,0:T(8,128)(2,1)}, u32[]{:S(2)}) copy-start(bf16[2,128,1024]{2,1,0:T(8,128)(2,1)} %param.6) | copy-start | bytes 1572868
  44.9 60.3 %all-gather.9.cloned.1.call-start = ((), (), s32[]{:S(2)}) async-start(), calls=%async_computation.1 | async-start | bytes 2359296 | tf_op jit(solution)/shard_map/all_gather | solution.py:23
  76.4 31.6 %copy-start.3 = (bf16[1024,1024]{1,0:T(8,128)(2,1)S(1)}, bf16[1024,1024]{1,0:T(8,128)(2,1)}, u32[]{:S(2)}) copy-start(bf16[1024,1024]{1,0:T(8,128)(2,1)} %param.9) | copy-start | bytes 6291460
  76.4 82.5 %all-gather.13.cloned.1.call-start = ((), (), s32[]{:S(2)}) async-start(), calls=%async_computation.3 | async-start | bytes 5242880 | tf_op jit(solution)/shard_map/all_gather | solution.py:28
  77.0 112.5 %all-gather.11.cloned.1.call-start = ((), (), s32[]{:S(2)}) async-start(), calls=%async_computation.2 | async-start | bytes 2359296 | tf_op jit(solution)/shard_map/all_gather | solution.py:25
  108.0 2.6 %copy-start.1 = (bf16[128,1024]{1,0:T(8,128)(2,1)S(1)}, bf16[128,1024]{1,0:T(8,128)(2,1)}, u32[]{:S(2)}) copy-start(bf16[128,1024]{1,0:T(8,128)(2,1)} %fusion.10) | copy-start | bytes 786436
  108.0 2.6 %copy-start.2 = (bf16[1024,128]{0,1:T(8,128)(2,1)S(1)}, bf16[1024,128]{0,1:T(8,128)(2,1)}, u32[]{:S(2)}) copy-start(bf16[1024,128]{0,1:T(8,128)(2,1)} %convolution_convert_fusion) | copy-start | bytes 786436
Sparse Core Ops, SparseCore 0:
  10.2 31.7 all-gather.14
  45.0 28.5 all-gather.6
  76.5 28.5 all-gather.8
  106.9 52.0 all-gather.12
  160.4 29.0 all-gather.10
where the time goes:
time: 207 us
  waiting for transfers between devices  169 us (82%)
  matrix products  16.9 us (8%)
  between operations  13.8 us (7%)
  local copies, waits for them, and re-layouts  6.89 us (3%)
    all_gather x1, waiting for transfers between devices, shards(): lax.all_gather(trailing_factor, 'col', axis=1, tiled=True)  47.6 us
    all_gather x1, waiting for transfers between devices, shards(): lax.all_gather(rhs_top[0], 'row', axis=0, tiled=True)  33 us
    all_gather x1, waiting for transfers between devices, shards(): second_all = lax.all_gather(second_mine, 'row', axis=0, tiled=True)  30.6 us
    all_gather x1, waiting for transfers between devices, shards(): first_all = lax.all_gather(first_mine, 'row', axis=0, tiled=True)  28.7 us
    all_gather x1, waiting for transfers between devices, shards(): lax.all_gather(carried, 'row', axis=0, tiled=True)  28.1 us
    dot_general x1, matrix products, shards(): jnp.dot(lax.all_gather(trailing_factor, 'col', axis=1, tiled=True), solut...  8.6 us
    dot_general x2, matrix products, fold_rows(): return jnp.dot(inverse_rows, piece, preferred_element_type=jnp.float32)  5.59 us
    unnamed x14, local copies, waits for them, and re-layouts  5.16 us
  transfers between devices with their start and end apart: 5, of which 5 were waited for; matrix products, arithmetic and copies ran while one was open for 3% of the time, Pallas kernels for 0%

commit v1 on v0

v1 whole, which is shorter than its diff:
```python
import functools

import jax
import jax.numpy as jnp
from jax import lax
from jax.experimental import pallas as pl
from jax.experimental.pallas import tpu as pltpu
from jax.sharding import PartitionSpec as P

VMEM_BYTES = 40 * 1024 * 1024


def bits_of(size):
    return [1 << b for b in reversed(range(size.bit_length() - 1))]


def send(x, sizes, to):
    rows, cols = sizes
    pairs = []
    for r in range(rows):
        for c in range(cols):
            there_r, there_c = to(r, c)
            pairs.append((r * cols + c, there_r * cols + there_c))
    return lax.ppermute(x, ("row", "col"), pairs)


def swap_cores(x, sizes):
    return send(x, sizes, lambda r, c: (r ^ 1, c))


def gather_line(x, sizes):
    chips = sizes[0] // 2
    held = {0: x}
    for bit in bits_of(chips):
        for s in list(held):
            held[s | bit] = send(held[s], sizes, lambda r, c: (r ^ (2 * bit), c))
    return [held[s] for s in range(chips)]


def plane_bits(cols, core):
    bits = bits_of(cols)
    return bits[::-1] if core == 0 else bits


def gather_plane(x, sizes):
    cols = sizes[1]
    held = [x]
    for i in range(len(bits_of(cols))):
        held += [
            send(h, sizes, lambda r, c: (r, c ^ plane_bits(cols, r % 2)[i])) for h in held
        ]
    return held


def plane_owner(c, m, cols, core):
    offsets = []
    for which in (0, 1):
        bits = plane_bits(cols, which)
        offsets.append(sum(bit for i, bit in enumerate(bits) if m >> i & 1))
    return c ^ jnp.where(core == 0, offsets[0], offsets[1])


def load_all(copies):
    for copy in copies:
        copy.start()
    for copy in copies:
        copy.wait()


def lower_product(inverse, right, out_ref, step):
    pb = inverse.shape[0]
    for top in range(0, pb, step):
        depth = top + step
        out_ref[top:depth, :] = jnp.dot(
            inverse[top:depth, :depth], right[:depth, :], preferred_element_type=jnp.float32
        ).astype(out_ref.dtype)


def inverse_copies(place, mine, theirs, inverse, sems, rows_dev, cols):
    z, k, c = place
    copies = []
    for packs, core in ((mine, k), (theirs, 1 - k)):
        for m, pack in enumerate(packs):
            owner = plane_owner(c, m, cols, core)
            chips, height, _ = pack.shape
            for s in range(chips):
                top = (z ^ s) * 2 * rows_dev + core * rows_dev + owner * height
                copies.append(
                    pltpu.make_async_copy(
                        pack.at[s],
                        inverse.at[pl.ds(pl.multiple_of(top, height), height), :],
                        sems.at[len(copies)],
                    )
                )
    return copies


def right_copies(place, blocks, right, sems, rows_dev, base):
    z, k, _ = place
    copies = []
    for s, block in enumerate(blocks):
        for part, core in ((0, k), (1, 1 - k)):
            top = (z ^ s) * 2 * rows_dev + core * rows_dev
            copies.append(
                pltpu.make_async_copy(
                    block.at[part * rows_dev : (part + 1) * rows_dev, :],
                    right.at[pl.ds(pl.multiple_of(top, rows_dev), rows_dev), :],
                    sems.at[base + len(copies)],
                )
            )
    return copies


def solve_kernel(chips, cols, rows_dev, carry, *refs):
    place_ref, refs = refs[0], refs[1:]
    place = tuple(place_ref[i] for i in range(3))
    mine, theirs, refs = refs[:cols], refs[cols : 2 * cols], refs[2 * cols :]
    blocks, refs = refs[:chips], refs[chips:]
    if carry:
        coupling, below, out_ref, carried_ref, inverse, right, sems = refs
    else:
        out_ref, inverse, right, sems = refs
    copies = inverse_copies(place, mine, theirs, inverse, sems, rows_dev, cols)
    copies += right_copies(place, blocks, right, sems, rows_dev, len(copies))
    load_all(copies)
    lower_product(inverse, right, out_ref, min(256, 2 * rows_dev))
    if carry:
        carried_ref[...] = (
            below[...].astype(jnp.float32)
            - jnp.dot(coupling[...], out_ref[...], preferred_element_type=jnp.float32)
        ).astype(carried_ref.dtype)


def solve(place, mine, theirs, blocks, sizes, rows_dev, pb, extra=()):
    chips, cols = sizes[0] // 2, sizes[1]
    width = blocks[0].shape[1]
    n_copies = 2 * cols * chips + 2 * chips
    any_spec = pl.BlockSpec(memory_space=pl.ANY)
    vmem = pl.BlockSpec(memory_space=pltpu.VMEM)
    out_shape = [jax.ShapeDtypeStruct((pb, width), jnp.bfloat16)]
    if extra:
        out_shape.append(jax.ShapeDtypeStruct((2 * rows_dev, width), jnp.bfloat16))
    return pl.pallas_call(
        functools.partial(solve_kernel, chips, cols, rows_dev, bool(extra)),
        out_shape=out_shape,
        in_specs=[pl.BlockSpec(memory_space=pltpu.SMEM)]
        + [any_spec] * (2 * cols + chips)
        + [vmem] * len(extra),
        out_specs=[vmem] * len(out_shape),
        scratch_shapes=[
            pltpu.VMEM((pb, pb), jnp.bfloat16),
            pltpu.VMEM((pb, width), jnp.bfloat16),
            pltpu.SemaphoreType.DMA((n_copies,)),
        ],
        compiler_params=pltpu.CompilerParams(vmem_limit_bytes=VMEM_BYTES),
    )(place, *mine, *theirs, *blocks, *extra)


def trailing_kernel(cols, rows_dev, place_ref, *refs):
    z, k, c = (place_ref[i] for i in range(3))
    factors, refs = refs[:cols], refs[cols:]
    x_mine, x_theirs, refs = refs[:2], refs[2:4], refs[4:]
    rhs, updated, solved, factor, x, sems = refs
    pb, width = x_mine[0].shape
    chunk = factors[0].shape[1]
    copies = []
    for m, block in enumerate(factors):
        left = pl.multiple_of(plane_owner(c, m, cols, k) * chunk, chunk)
        copies.append(
            pltpu.make_async_copy(block, factor.at[:, pl.ds(left, chunk)], sems.at[len(copies)])
        )
    for parts, core in ((x_mine, k), (x_theirs, 1 - k)):
        left = pl.multiple_of(core * width, width)
        for panel, part in enumerate(parts):
            copies.append(
                pltpu.make_async_copy(
                    part,
                    x.at[panel * pb : (panel + 1) * pb, pl.ds(left, width)],
                    sems.at[len(copies)],
                )
            )
    load_all(copies)
    top = pl.multiple_of((2 * z + k) * rows_dev, rows_dev)
    for panel in range(2):
        solved[panel] = x[pl.ds(panel * pb + top, rows_dev), :]
    step = min(256, rhs.shape[0])
    for at in range(0, rhs.shape[0], step):
        updated[at : at + step, :] = (
            rhs[at : at + step, :].astype(jnp.float32)
            - jnp.dot(factor[at : at + step, :], x[...], preferred_element_type=jnp.float32)
        ).astype(updated.dtype)


def trailing(place, factors, x_mine, x_theirs, rhs, rows_dev):
    cols = len(factors)
    pb, width = x_mine[0].shape
    any_spec = pl.BlockSpec(memory_space=pl.ANY)
    vmem = pl.BlockSpec(memory_space=pltpu.VMEM)
    return pl.pallas_call(
        functools.partial(trailing_kernel, cols, rows_dev),
        out_shape=[
            jax.ShapeDtypeStruct(rhs.shape, jnp.bfloat16),
            jax.ShapeDtypeStruct((2, rows_dev, 2 * width), jnp.bfloat16),
        ],
        in_specs=[pl.BlockSpec(memory_space=pltpu.SMEM)] + [any_spec] * (cols + 4) + [vmem],
        out_specs=[vmem, vmem],
        scratch_shapes=[
            pltpu.VMEM((rhs.shape[0], cols * factors[0].shape[1]), jnp.bfloat16),
            pltpu.VMEM((2 * pb, 2 * width), jnp.bfloat16),
            pltpu.SemaphoreType.DMA((cols + 4,)),
        ],
        compiler_params=pltpu.CompilerParams(vmem_limit_bytes=VMEM_BYTES),
    )(place, *factors, *x_mine, *x_theirs, rhs)


def by_permutes(sizes, rhs_top, diag_inverse, panel_coupling, trailing_factor, rhs_trailing):
    rows, cols = sizes
    rows_dev, pb = diag_inverse.shape[1:]
    half = rhs_top.shape[2] // 2
    r, c = lax.axis_index("row"), lax.axis_index("col")
    z, k = r // 2, r % 2
    place = jnp.stack([z, k, c]).astype(jnp.int32)

    mine = lax.dynamic_slice_in_dim(rhs_top, k * half, half, 2)
    theirs = swap_cores(lax.dynamic_slice_in_dim(rhs_top, (1 - k) * half, half, 2), sizes)
    chip_rhs = jnp.concatenate([mine, theirs], axis=1)
    chip_coupling = jnp.concatenate([panel_coupling, swap_cores(panel_coupling, sizes)], axis=0)

    height = rows_dev // cols
    share = lax.dynamic_slice_in_dim(diag_inverse, c * height, height, 1)
    packs, their_packs = [], []
    for panel in range(2):
        pack = jnp.stack(gather_line(share[panel], sizes))
        packs.append(gather_plane(pack, sizes))
        their_packs.append([swap_cores(p, sizes) for p in packs[-1]])
    factors = gather_plane(trailing_factor, sizes)

    blocks = gather_line(chip_rhs[0], sizes)
    first, carried = solve(
        place, packs[0], their_packs[0], blocks, sizes, rows_dev, pb, (chip_coupling, chip_rhs[1])
    )
    first_theirs = swap_cores(first, sizes)
    blocks = gather_line(carried, sizes)
    (second,) = solve(place, packs[1], their_packs[1], blocks, sizes, rows_dev, pb)
    second_theirs = swap_cores(second, sizes)
    updated, solved = trailing(
        place, factors, (first, second), (first_theirs, second_theirs), rhs_trailing, rows_dev
    )
    return solved, updated


def by_gathers(rhs_top, diag_inverse, panel_coupling, trailing_factor, rhs_trailing):
    def product(left, right):
        return jnp.dot(left, right, preferred_element_type=jnp.float32)

    def whole(x):
        return lax.all_gather(x, "row", axis=0, tiled=True)

    first = product(diag_inverse[0], whole(rhs_top[0])).astype(jnp.bfloat16)
    first_all = whole(first)
    carried = rhs_top[1].astype(jnp.float32) - product(panel_coupling, first_all)
    second = product(diag_inverse[1], whole(carried.astype(jnp.bfloat16))).astype(jnp.bfloat16)
    x = jnp.concatenate([first_all, whole(second)], axis=0)
    factor = lax.all_gather(trailing_factor, "col", axis=1, tiled=True)
    updated = (rhs_trailing.astype(jnp.float32) - product(factor, x)).astype(jnp.bfloat16)
    return jnp.stack([first, second]), updated


def fits(sizes, rhs_top, diag_inverse):
    rows, cols = sizes
    powers = rows >= 2 and rows & (rows - 1) == 0 and cols & (cols - 1) == 0
    return powers and diag_inverse.shape[1] % (16 * cols) == 0 and rhs_top.shape[2] % 256 == 0


def solution(mesh):
    sizes = (mesh.shape["row"], mesh.shape["col"])

    def shards(rhs_top, diag_inverse, *others):
        if fits(sizes, rhs_top, diag_inverse):
            return by_permutes(sizes, rhs_top, diag_inverse, *others)
        return by_gathers(rhs_top, diag_inverse, *others)

    in_specs = (
        P(None, "row", "col"),
        P(None, "row", None),
        P("row", None),
        P("row", "col"),
        P("row", "col"),
    )
    out_specs = (P(None, "row", "col"), P("row", "col"))
    return jax.shard_map(shards, mesh=mesh, in_specs=in_specs, out_specs=out_specs, check_vma=False)
```

time: 207 us -> 103 us (0.50)
  waiting for transfers between devices: 169 us -> 42.3 us
  starting transfers between devices: 0.2 us -> 33.6 us
  Pallas kernels: 0 us -> 19.1 us
  matrix products: 16.9 us -> 0 us
  between operations: 13.8 us -> 0.8 us
    all_gather x5 -> x0, waiting for transfers between devices: 168 us -> none  [the longest x1 47.6 us: shards(): lax.all_gather(trailing_factor, 'col', axis=1, tiled=True)]
    ppermute x0 -> x33, waiting for transfers between devices: none -> 42.3 us  [send(): return lax.ppermute(x, ('row', 'col'), pairs)]
    ppermute x0 -> x33, starting transfers between devices: none -> 33.6 us  [send(): return lax.ppermute(x, ('row', 'col'), pairs)]
    pallas_call x0 -> x3, Pallas kernels: none -> 19.1 us  [the longest x2 11.4 us: solve(): pl.pallas_call(functools.partial(solve_kernel, chips, cols, rows_dev, boo...]
    dot_general x4 -> x0, matrix products: 16.9 us -> none  [the longest x1 8.6 us: shards(): jnp.dot(lax.all_gather(trailing_factor, 'col', axis=1, tiled=True), solut...]
    unnamed x14 -> x18, local copies, waits for them, and re-layouts: 5.16 us -> 3.32 us
  transfers between devices with their start and end apart: 5 -> 33, of which waited for: 5 -> 12; matrix products, arithmetic and copies ran while one was open for 3% -> 2% of each run, Pallas kernels for 0% -> 11%
where the time goes in v1:
time: 103 us; the launch traced here: 102 us
  waiting for transfers between devices  42.3 us (41%)
  starting transfers between devices  33.6 us (33%)
  Pallas kernels  19.1 us (19%)
  local copies, waits for them, and re-layouts  5.35 us (5%)
  other arithmetic  1.25 us (1%)
    ppermute x33, waiting for transfers between devices, send(): return lax.ppermute(x, ('row', 'col'), pairs)  42.3 us
    ppermute x33, starting transfers between devices, send(): return lax.ppermute(x, ('row', 'col'), pairs)  33.6 us
    pallas_call x2, Pallas kernels, solve(): pl.pallas_call(functools.partial(solve_kernel, chips, cols, rows_dev, boo...  11.4 us
    pallas_call x1, Pallas kernels, trailing(): pl.pallas_call(functools.partial(trailing_kernel, cols, rows_dev), out_sh...  7.72 us
    unnamed x18, local copies, waits for them, and re-layouts  3.32 us
  transfers between devices with their start and end apart: 33, of which 12 were waited for; matrix products, arithmetic and copies ran while one was open for 2% of the time, Pallas kernels for 11%

profile of v1, /device:TPU:0, one launch (start us, length us, event | category | flops | bytes accessed | tf_op | source)
XLA Modules:
  0.0 102.3 jit_solution(16120623149820767682)
XLA Ops:
  0.6 1.0 constant_dynamic-slice_fusion.3
  1.6 4.1 %collective-permute-start.19 = (bf16[32,1024]{1,0:T(8,128)(2,1)S(1)}, bf16[32,1024]{1,0:T(8,128)(2,1)S(1)}, u32[]{:S(2)}, u32[]{:S(2)}) collective-permute-start(bf16[32,1024]{1,0:T(8,128)(2,1)S(1)} %bitcast.17), channel_id=1, source_target_pairs={{0,16},{1,17},{2,18},{3,19},{4,20},{5,21},{6,22},{7,23},{8,24},{9,... | collective-permute-start | bytes 196616 | tf_op jit(solution)/shard_map/ppermute | solution.py:24
  5.7 1.6 %collective-permute-start.18 = (bf16[32,1024]{1,0:T(8,128)(2,1)S(1)}, bf16[32,1024]{1,0:T(8,128)(2,1)S(1)}, u32[]{:S(2)}, u32[]{:S(2)}) collective-permute-start(bf16[32,1024]{1,0:T(8,128)(2,1)S(1)} %bitcast.18), channel_id=1, source_target_pairs={{0,8},{1,9},{2,10},{3,11},{4,12},{5,13},{6,14},{7,15},{8,0},{9,1},... | collective-permute-start | bytes 196616 | tf_op jit(solution)/shard_map/ppermute | solution.py:24
  7.3 0.3 collective-permute-start.4
  7.6 1.1 %collective-permute-done.19 = bf16[32,1024]{1,0:T(8,128)(2,1)S(1)} collective-permute-done((bf16[32,1024]{1,0:T(8,128)(2,1)S(1)}, bf16[32,1024]{1,0:T(8,128)(2,1)S(1)}, u32[]{:S(2)}, u32[]{:S(2)}) %collective-permute-start.19) | collective-permute-done | bytes 65568 | tf_op jit(solution)/shard_map/ppermute | solution.py:24
  8.8 2.1 %collective-permute-start.20 = (bf16[32,1024]{1,0:T(8,128)(2,1)S(1)}, bf16[32,1024]{1,0:T(8,128)(2,1)S(1)}, u32[]{:S(2)}, u32[]{:S(2)}) collective-permute-start(bf16[32,1024]{1,0:T(8,128)(2,1)S(1)} %collective-permute-done.19), channel_id=1, source_target_pairs={{0,8},{1,9},{2,10},{3,11},{4,12},{5,13},{6,14},{7,15},{8,0},{9,1},... | collective-permute-start | bytes 196616 | tf_op jit(solution)/shard_map/ppermute | solution.py:24
  10.8 1.1 %constant_dynamic-slice_fusion.1 = (bf16[2,128,512]{2,1,0:T(8,128)(2,1)S(1)}, bf16[2,128,512]{2,1,0:T(8,128)(2,1)S(1)}) fusion(bf16[2,128,1024]{2,1,0:T(8,128)(2,1)} %param.5, s32[]{:T(128)S(6)} %select_n.24, s32[]{:T(128)S(6)} %select_n.23), kind=kLoop, calls=%fused_computation.10 | loop fusion | bytes 1048584 | tf_op jit(solution)/shard_map/dynamic_slice | solution.py:225
  11.9 0.1 collective-permute-start.13
  12.0 0.1 collective-permute-start.3
  12.1 1.1 %collective-permute-done.4 = bf16[32,1024]{1,0:T(8,128)(2,1)S(1)} collective-permute-done((bf16[32,1024]{1,0:T(8,128)(2,1)S(1)}, bf16[32,1024]{1,0:T(8,128)(2,1)S(1)}, u32[]{:S(2)}, u32[]{:S(2)}) %collective-permute-start.4) | collective-permute-done | bytes 65568 | tf_op jit(solution)/shard_map/ppermute | solution.py:24
  13.2 0.0 collective-permute-start.17
  13.2 0.0 collective-permute-done.18
  13.2 1.1 %collective-permute-start.5 = (bf16[32,1024]{1,0:T(8,128)(2,1)S(1)}, bf16[32,1024]{1,0:T(8,128)(2,1)S(1)}, u32[]{:S(2)}, u32[]{:S(2)}) collective-permute-start(bf16[32,1024]{1,0:T(8,128)(2,1)S(1)} %collective-permute-done.4), channel_id=1, source_target_pairs={{0,8},{1,9},{2,10},{3,11},{4,12},{5,13},{6,14},{7,15},{8,0},{9,1},... | collective-permute-start | bytes 196616 | tf_op jit(solution)/shard_map/ppermute | solution.py:24
  14.2 0.0 collective-permute-done.20
  14.3 1.6 %collective-permute-start.22 = (bf16[4,32,1024]{2,1,0:T(8,128)(2,1)S(1)}, bf16[4,32,1024]{2,1,0:T(8,128)(2,1)S(1)}, u32[]{:S(2)}, u32[]{:S(2)}) collective-permute-start(bf16[4,32,1024]{2,1,0:T(8,128)(2,1)S(1)} %pad_maximum_fusion.3.refs_1_), channel_id=1, source_target_pairs={{0,2},{1,3},{2,0},{3,1},{4,5},{5,4},{6,7},{7,6},{8,10},{9,11},{10,... | collective-permute-start | bytes 786440 | tf_op jit(solution)/shard_map/ppermute | solution.py:24
  15.9 0.9 collective-permute-done.3
  16.8 1.6 %collective-permute-start.21 = (bf16[4,32,1024]{2,1,0:T(8,128)(2,1)S(1)}, bf16[4,32,1024]{2,1,0:T(8,128)(2,1)S(1)}, u32[]{:S(2)}, u32[]{:S(2)}) collective-permute-start(bf16[4,32,1024]{2,1,0:T(8,128)(2,1)S(1)} %pad_maximum_fusion.3.refs_1_), channel_id=1, source_target_pairs={{0,1},{1,0},{2,3},{3,2},{4,6},{5,7},{6,4},{7,5},{8,9},{9,8},{10,11... | collective-permute-start | bytes 786440 | tf_op jit(solution)/shard_map/ppermute | solution.py:24
  18.4 1.1 %collective-permute-start.6 = (bf16[4,32,1024]{2,1,0:T(8,128)(2,1)S(1)}, bf16[4,32,1024]{2,1,0:T(8,128)(2,1)}, u32[]{:S(2)}, u32[]{:S(2)}) collective-permute-start(bf16[4,32,1024]{2,1,0:T(8,128)(2,1)S(1)} %pad_maximum_fusion.2.refs_1_), channel_id=1, source_target_pairs={{0,1},{1,0},{2,3},{3,2},{4,6},{5,7},{6,4},{7,5},{8,9},{9,8},{10,11... | collective-permute-start | bytes 786440 | tf_op jit(solution)/shard_map/ppermute | solution.py:24
  19.5 0.0 collective-permute-done.13
  19.5 0.0 collective-permute-start.9
  19.6 1.6 %collective-permute-start.7 = (bf16[4,32,1024]{2,1,0:T(8,128)(2,1)S(1)}, bf16[4,32,1024]{2,1,0:T(8,128)(2,1)}, u32[]{:S(2)}, u32[]{:S(2)}) collective-permute-start(bf16[4,32,1024]{2,1,0:T(8,128)(2,1)S(1)} %pad_maximum_fusion.2.refs_1_), channel_id=1, source_target_pairs={{0,2},{1,3},{2,0},{3,1},{4,5},{5,4},{6,7},{7,6},{8,10},{9,11},{10,... | collective-permute-start | bytes 786440 | tf_op jit(solution)/shard_map/ppermute | solution.py:24
  21.1 1.6 %collective-permute-done.22.refs_3_ = bf16[4,32,1024]{2,1,0:T(8,128)(2,1)S(1)} collective-permute-done((bf16[4,32,1024]{2,1,0:T(8,128)(2,1)S(1)}, bf16[4,32,1024]{2,1,0:T(8,128)(2,1)S(1)}, u32[]{:S(2)}, u32[]{:S(2)}) %collective-permute-start.22) | collective-permute-done | bytes 262176 | tf_op jit(solution)/shard_map/ppermute | solution.py:24
  22.7 3.6 %collective-permute-start.15 = (bf16[256,512]{1,0:T(8,128)(2,1)S(1)}, bf16[256,512]{1,0:T(8,128)(2,1)}, u32[]{:S(2)}, u32[]{:S(2)}) collective-permute-start(bf16[256,512]{1,0:T(8,128)(2,1)S(1)} %get-tuple-element.13.refs_9_), channel_id=1, source_target_pairs={{0,16},{1,17},{2,18},{3,19},{4,20},{5,21},{6,22},{7,23},{8,24},{9,... | collective-permute-start | bytes 786440 | tf_op jit(solution)/shard_map/ppermute | solution.py:24
  26.4 0.0 collective-permute-done.21.refs_2_
  26.4 1.3 %collective-permute-start.14 = (bf16[256,512]{1,0:T(8,128)(2,1)S(1)}, bf16[256,512]{1,0:T(8,128)(2,1)S(1)}, u32[]{:S(2)}, u32[]{:S(2)}) collective-permute-start(bf16[256,512]{1,0:T(8,128)(2,1)S(1)} %get-tuple-element.13.refs_9_), channel_id=1, source_target_pairs={{0,8},{1,9},{2,10},{3,11},{4,12},{5,13},{6,14},{7,15},{8,0},{9,1},... | collective-permute-start | bytes 786440 | tf_op jit(solution)/shard_map/ppermute | solution.py:24
  27.7 1.2 %collective-permute-done.6.refs_2_ = bf16[4,32,1024]{2,1,0:T(8,128)(2,1)} collective-permute-done((bf16[4,32,1024]{2,1,0:T(8,128)(2,1)S(1)}, bf16[4,32,1024]{2,1,0:T(8,128)(2,1)}, u32[]{:S(2)}, u32[]{:S(2)}) %collective-permute-start.6) | collective-permute-done | bytes 262176 | tf_op jit(solution)/shard_map/ppermute | solution.py:24
  28.8 1.6 %collective-permute-start.8 = (bf16[4,32,1024]{2,1,0:T(8,128)(2,1)}, bf16[4,32,1024]{2,1,0:T(8,128)(2,1)}, u32[]{:S(2)}, u32[]{:S(2)}) collective-permute-start(bf16[4,32,1024]{2,1,0:T(8,128)(2,1)} %collective-permute-done.6.refs_2_), channel_id=1, source_target_pairs={{0,2},{1,3},{2,0},{3,1},{4,5},{5,4},{6,7},{7,6},{8,10},{9,11},{10,... | collective-permute-start | bytes 786440 | tf_op jit(solution)/shard_map/ppermute | solution.py:24
  30.5 0.0 copy-start.4
  30.5 0.7 copy-done.4
  31.2 1.5 %collective-permute-start = (bf16[1024,512]{1,0:T(8,128)(2,1)S(1)}, bf16[1024,512]{1,0:T(8,128)(2,1)S(1)}, u32[]{:S(2)}, u32[]{:S(2)}) collective-permute-start(bf16[1024,512]{1,0:T(8,128)(2,1)S(1)} %copy-done.1), channel_id=1, source_target_pairs={{0,1},{1,0},{2,3},{3,2},{4,6},{5,7},{6,4},{7,5},{8,9},{9,8},{10,11... | collective-permute-start | bytes 3145736 | tf_op jit(solution)/shard_map/ppermute | solution.py:24
  32.7 0.0 collective-permute-done.7.refs_3_
  32.7 0.0 collective-permute-start.11
  32.7 3.8 %collective-permute-done.15.refs_11_ = bf16[256,512]{1,0:T(8,128)(2,1)} collective-permute-done((bf16[256,512]{1,0:T(8,128)(2,1)S(1)}, bf16[256,512]{1,0:T(8,128)(2,1)}, u32[]{:S(2)}, u32[]{:S(2)}) %collective-permute-start.15) | collective-permute-done | bytes 262176 | tf_op jit(solution)/shard_map/ppermute | solution.py:24
  36.4 0.0 collective-permute-start.10
  36.5 1.6 %collective-permute-done.14.refs_10_ = bf16[256,512]{1,0:T(8,128)(2,1)S(1)} collective-permute-done((bf16[256,512]{1,0:T(8,128)(2,1)S(1)}, bf16[256,512]{1,0:T(8,128)(2,1)S(1)}, u32[]{:S(2)}, u32[]{:S(2)}) %collective-permute-start.14) | collective-permute-done | bytes 262176 | tf_op jit(solution)/shard_map/ppermute | solution.py:24
  38.0 0.7 copy-done.6
  38.7 0.4 collective-permute-start.16
  39.1 0.0 collective-permute-start.12
  39.1 0.1 pad_add_fusion.refs_0_.place_ref
  39.2 1.1 %pad_maximum_fusion.refs_13_ = bf16[256,1024]{1,0:T(8,128)(2,1)S(1)} fusion(bf16[128,1024]{1,0:T(8,128)(2,1)} %copy-done.8, bf16[128,1024]{1,0:T(8,128)(2,1)} %param.7), kind=kLoop, calls=%fused_computation.2 | loop fusion | flops 1048576 | bytes 1048576 | tf_op jit(solution)/shard_map/concatenate | solution.py:227
  40.3 0.6 collective-permute-start.24
  40.9 0.0 collective-permute-done.10.refs_6_
  40.9 1.5 %collective-permute-start.23 = (bf16[4,32,1024]{2,1,0:T(8,128)(2,1)}, bf16[4,32,1024]{2,1,0:T(8,128)(2,1)S(1)}, u32[]{:S(2)}, u32[]{:S(2)}) collective-permute-start(bf16[4,32,1024]{2,1,0:T(8,128)(2,1)} %copy-done.2), channel_id=1, source_target_pairs={{0,2},{1,3},{2,0},{3,1},{4,5},{5,4},{6,7},{7,6},{8,10},{9,11},{10,... | collective-permute-start | bytes 786440 | tf_op jit(solution)/shard_map/ppermute | solution.py:24
  42.4 3.8 %collective-permute-done.16.refs_12_ = bf16[256,512]{1,0:T(8,128)(2,1)} collective-permute-done((bf16[256,512]{1,0:T(8,128)(2,1)}, bf16[256,512]{1,0:T(8,128)(2,1)}, u32[]{:S(2)}, u32[]{:S(2)}) %collective-permute-start.16) | collective-permute-done | bytes 262176 | tf_op jit(solution)/shard_map/ppermute | solution.py:24
  46.2 0.0 collective-permute-start.26
  46.2 0.9 copy-done.5
  47.2 0.9 copy-done.7
  48.1 4.7 %shard_map.68 = (bf16[1024,512]{1,0:T(8,128)(2,1)S(1)}, bf16[256,512]{1,0:T(8,128)(2,1)S(1)}) custom-call(s32[3]{0:T(128)S(1)} %pad_add_fusion.refs_0_.place_ref, bf16[4,32,1024]{2,1,0:T(8,128)(2,1)S(1)} %pad_maximum_fusion.2.refs_1_, bf16[4,32,1024]{2,1,0:T(8,128)(2,1)} %collective-permute-done.6.refs_2_, ...), custom_call_target="tpu_custom_call" | custom-call | tf_op jit(solution)/shard_map/pallas_call | solution.py:143
  52.9 2.4 %collective-permute-start.29 = (bf16[256,512]{1,0:T(8,128)(2,1)S(1)}, bf16[256,512]{1,0:T(8,128)(2,1)S(1)}, u32[]{:S(2)}, u32[]{:S(2)}) collective-permute-start(bf16[256,512]{1,0:T(8,128)(2,1)S(1)} %get-tuple-element.7.refs_9_), channel_id=1, source_target_pairs={{0,16},{1,17},{2,18},{3,19},{4,20},{5,21},{6,22},{7,23},{8,24},{9,... | collective-permute-start | bytes 786440 | tf_op jit(solution)/shard_map/ppermute | solution.py:24
  55.2 0.2 collective-permute-start.25
  55.5 0.0 collective-permute-done.23.refs_4_
  55.5 0.3 collective-permute-start.27
  55.7 1.7 %collective-permute-start.28 = (bf16[256,512]{1,0:T(8,128)(2,1)S(1)}, bf16[256,512]{1,0:T(8,128)(2,1)S(1)}, u32[]{:S(2)}, u32[]{:S(2)}) collective-permute-start(bf16[256,512]{1,0:T(8,128)(2,1)S(1)} %get-tuple-element.7.refs_9_), channel_id=1, source_target_pairs={{0,8},{1,9},{2,10},{3,11},{4,12},{5,13},{6,14},{7,15},{8,0},{9,1},... | collective-permute-start | bytes 786440 | tf_op jit(solution)/shard_map/ppermute | solution.py:24
  57.5 10.8 %collective-permute-done.29.refs_11_ = bf16[256,512]{1,0:T(8,128)(2,1)S(1)} collective-permute-done((bf16[256,512]{1,0:T(8,128)(2,1)S(1)}, bf16[256,512]{1,0:T(8,128)(2,1)S(1)}, u32[]{:S(2)}, u32[]{:S(2)}) %collective-permute-start.29) | collective-permute-done | bytes 262176 | tf_op jit(solution)/shard_map/ppermute | solution.py:24
  68.3 0.3 collective-permute-start.30
  68.6 0.0 collective-permute-done.25.refs_6_
  68.6 1.5 %collective-permute-start.1 = (bf16[1024,512]{1,0:T(8,128)(2,1)S(1)}, bf16[1024,512]{1,0:T(8,128)(2,1)S(1)}, u32[]{:S(2)}, u32[]{:S(2)}) collective-permute-start(bf16[1024,512]{1,0:T(8,128)(2,1)S(1)} %copy-done.1), channel_id=1, source_target_pairs={{0,2},{1,3},{2,0},{3,1},{4,5},{5,4},{6,7},{7,6},{8,10},{9,11},{10,... | collective-permute-start | bytes 3145736 | tf_op jit(solution)/shard_map/ppermute | solution.py:24
  70.1 1.4 %collective-permute-start.2 = (bf16[1024,512]{1,0:T(8,128)(2,1)S(1)}, bf16[1024,512]{1,0:T(8,128)(2,1)S(1)}, u32[]{:S(2)}, u32[]{:S(2)}) collective-permute-start(bf16[1024,512]{1,0:T(8,128)(2,1)S(1)} %collective-permute-done.refs_1_), channel_id=1, source_target_pairs={{0,2},{1,3},{2,0},{3,1},{4,5},{5,4},{6,7},{7,6},{8,10},{9,11},{10,... | collective-permute-start | bytes 3145736 | tf_op jit(solution)/shard_map/ppermute | solution.py:24
  71.5 4.7 %collective-permute-done.30.refs_12_ = bf16[256,512]{1,0:T(8,128)(2,1)S(1)} collective-permute-done((bf16[256,512]{1,0:T(8,128)(2,1)S(1)}, bf16[256,512]{1,0:T(8,128)(2,1)S(1)}, u32[]{:S(2)}, u32[]{:S(2)}) %collective-permute-start.30) | collective-permute-done | bytes 262176 | tf_op jit(solution)/shard_map/ppermute | solution.py:24
  76.1 6.6 %shard_map.69.refs_5_ = bf16[1024,512]{1,0:T(8,128)(2,1)S(1)} custom-call(s32[3]{0:T(128)S(1)} %pad_add_fusion.refs_0_.place_ref, bf16[4,32,1024]{2,1,0:T(8,128)(2,1)S(1)} %pad_maximum_fusion.3.refs_1_, bf16[4,32,1024]{2,1,0:T(8,128)(2,1)S(1)} %copy-done.3, bf16[4,32,1024]{2,1,0:T(8,128)(2,1)S(1)} %collective-permute-done.22.refs_3_, ...), custom_call_target="tpu_custom_call" | custom-call | tf_op jit(solution)/shard_map/pallas_call | solution.py:143
  82.8 0.1 collective-permute-start.32
  82.9 0.5 collective-permute-done.1.refs_2_
  83.4 11.2 %collective-permute-done.2.refs_3_ = bf16[1024,512]{1,0:T(8,128)(2,1)S(1)} collective-permute-done((bf16[1024,512]{1,0:T(8,128)(2,1)S(1)}, bf16[1024,512]{1,0:T(8,128)(2,1)S(1)}, u32[]{:S(2)}, u32[]{:S(2)}) %collective-permute-start.2) | collective-permute-done | bytes 1048608 | tf_op jit(solution)/shard_map/ppermute | solution.py:24
  94.6 7.7 %shard_map.70 = (bf16[1024,1024]{1,0:T(8,128)(2,1)}, bf16[2,128,1024]{2,1,0:T(8,128)(2,1)}) custom-call(s32[3]{0:T(128)S(1)} %pad_add_fusion.refs_0_.place_ref, bf16[1024,512]{1,0:T(8,128)(2,1)S(1)} %copy-done.1, bf16[1024,512]{1,0:T(8,128)(2,1)S(1)} %collective-permute-done.refs_1_, bf16[1024,512]{1,0:T(8,128)(2,1)S(1)} %collective-permute-done.1.refs_2_, ...), custom_call_target="tpu_custom_call" | custom-call | tf_op jit(solution)/shard_map/pallas_call | solution.py:199
  (30 shorter events, 0.2 us)
Async XLA Ops:
  0.6 30.5 %copy-start.1 = (bf16[1024,512]{1,0:T(8,128)(2,1)S(1)}, bf16[1024,512]{1,0:T(8,128)(2,1)}, u32[]{:S(2)}) copy-start(bf16[1024,512]{1,0:T(8,128)(2,1)} %refs_0_.1) | copy-start | bytes 3145732
  1.6 7.2 %collective-permute-start.19 = (bf16[32,1024]{1,0:T(8,128)(2,1)S(1)}, bf16[32,1024]{1,0:T(8,128)(2,1)S(1)}, u32[]{:S(2)}, u32[]{:S(2)}) collective-permute-start(bf16[32,1024]{1,0:T(8,128)(2,1)S(1)} %bitcast.17), channel_id=1, source_target_pairs={{0,16},{1,17},{2,18},{3,19},{4,20},{5,21},{6,22},{7,23},{8,24},{9,... | collective-permute-start | bytes 196616 | tf_op jit(solution)/shard_map/ppermute | solution.py:24
  5.7 7.4 %collective-permute-start.18 = (bf16[32,1024]{1,0:T(8,128)(2,1)S(1)}, bf16[32,1024]{1,0:T(8,128)(2,1)S(1)}, u32[]{:S(2)}, u32[]{:S(2)}) collective-permute-start(bf16[32,1024]{1,0:T(8,128)(2,1)S(1)} %bitcast.18), channel_id=1, source_target_pairs={{0,8},{1,9},{2,10},{3,11},{4,12},{5,13},{6,14},{7,15},{8,0},{9,1},... | collective-permute-start | bytes 196616 | tf_op jit(solution)/shard_map/ppermute | solution.py:24
  7.3 5.9 %collective-permute-start.4 = (bf16[32,1024]{1,0:T(8,128)(2,1)S(1)}, bf16[32,1024]{1,0:T(8,128)(2,1)S(1)}, u32[]{:S(2)}, u32[]{:S(2)}) collective-permute-start(bf16[32,1024]{1,0:T(8,128)(2,1)S(1)} %bitcast.15), channel_id=1, source_target_pairs={{0,16},{1,17},{2,18},{3,19},{4,20},{5,21},{6,22},{7,23},{8,24},{9,... | collective-permute-start | bytes 196616 | tf_op jit(solution)/shard_map/ppermute | solution.py:24
  8.8 5.5 %collective-permute-start.20 = (bf16[32,1024]{1,0:T(8,128)(2,1)S(1)}, bf16[32,1024]{1,0:T(8,128)(2,1)S(1)}, u32[]{:S(2)}, u32[]{:S(2)}) collective-permute-start(bf16[32,1024]{1,0:T(8,128)(2,1)S(1)} %collective-permute-done.19), channel_id=1, source_target_pairs={{0,8},{1,9},{2,10},{3,11},{4,12},{5,13},{6,14},{7,15},{8,0},{9,1},... | collective-permute-start | bytes 196616 | tf_op jit(solution)/shard_map/ppermute | solution.py:24
  11.9 7.6 %collective-permute-start.13 = (bf16[2,128,512]{2,1,0:T(8,128)(2,1)S(1)}, bf16[2,128,512]{2,1,0:T(8,128)(2,1)S(1)}, u32[]{:S(2)}, u32[]{:S(2)}) collective-permute-start(bf16[2,128,512]{2,1,0:T(8,128)(2,1)S(1)} %get-tuple-element.14), channel_id=1, source_target_pairs={{0,4},{1,5},{2,6},{3,7},{4,0},{5,1},{6,2},{7,3},{8,12},{9,13},{10,... | collective-permute-start | bytes 786440 | tf_op jit(solution)/shard_map/ppermute | solution.py:24
  12.0 4.8 %collective-permute-start.3 = (bf16[32,1024]{1,0:T(8,128)(2,1)S(1)}, bf16[32,1024]{1,0:T(8,128)(2,1)S(1)}, u32[]{:S(2)}, u32[]{:S(2)}) collective-permute-start(bf16[32,1024]{1,0:T(8,128)(2,1)S(1)} %bitcast.16), channel_id=1, source_target_pairs={{0,8},{1,9},{2,10},{3,11},{4,12},{5,13},{6,14},{7,15},{8,0},{9,1},... | collective-permute-start | bytes 196616 | tf_op jit(solution)/shard_map/ppermute | solution.py:24
  13.2 6.4 %collective-permute-start.17 = (bf16[128,1024]{1,0:T(8,128)(2,1)}, bf16[128,1024]{1,0:T(8,128)(2,1)S(1)}, u32[]{:S(2)}, u32[]{:S(2)}) collective-permute-start(bf16[128,1024]{1,0:T(8,128)(2,1)} %param.7), channel_id=1, source_target_pairs={{0,4},{1,5},{2,6},{3,7},{4,0},{5,1},{6,2},{7,3},{8,12},{9,13},{10,... | collective-permute-start | bytes 786440 | tf_op jit(solution)/shard_map/ppermute | solution.py:24
  13.2 5.2 %collective-permute-start.5 = (bf16[32,1024]{1,0:T(8,128)(2,1)S(1)}, bf16[32,1024]{1,0:T(8,128)(2,1)S(1)}, u32[]{:S(2)}, u32[]{:S(2)}) collective-permute-start(bf16[32,1024]{1,0:T(8,128)(2,1)S(1)} %collective-permute-done.4), channel_id=1, source_target_pairs={{0,8},{1,9},{2,10},{3,11},{4,12},{5,13},{6,14},{7,15},{8,0},{9,1},... | collective-permute-start | bytes 196616 | tf_op jit(solution)/shard_map/ppermute | solution.py:24
  14.3 8.4 %collective-permute-start.22 = (bf16[4,32,1024]{2,1,0:T(8,128)(2,1)S(1)}, bf16[4,32,1024]{2,1,0:T(8,128)(2,1)S(1)}, u32[]{:S(2)}, u32[]{:S(2)}) collective-permute-start(bf16[4,32,1024]{2,1,0:T(8,128)(2,1)S(1)} %pad_maximum_fusion.3.refs_1_), channel_id=1, source_target_pairs={{0,2},{1,3},{2,0},{3,1},{4,5},{5,4},{6,7},{7,6},{8,10},{9,11},{10,... | collective-permute-start | bytes 786440 | tf_op jit(solution)/shard_map/ppermute | solution.py:24
  16.8 9.6 %collective-permute-start.21 = (bf16[4,32,1024]{2,1,0:T(8,128)(2,1)S(1)}, bf16[4,32,1024]{2,1,0:T(8,128)(2,1)S(1)}, u32[]{:S(2)}, u32[]{:S(2)}) collective-permute-start(bf16[4,32,1024]{2,1,0:T(8,128)(2,1)S(1)} %pad_maximum_fusion.3.refs_1_), channel_id=1, source_target_pairs={{0,1},{1,0},{2,3},{3,2},{4,6},{5,7},{6,4},{7,5},{8,9},{9,8},{10,11... | collective-permute-start | bytes 786440 | tf_op jit(solution)/shard_map/ppermute | solution.py:24
  18.4 10.5 %collective-permute-start.6 = (bf16[4,32,1024]{2,1,0:T(8,128)(2,1)S(1)}, bf16[4,32,1024]{2,1,0:T(8,128)(2,1)}, u32[]{:S(2)}, u32[]{:S(2)}) collective-permute-start(bf16[4,32,1024]{2,1,0:T(8,128)(2,1)S(1)} %pad_maximum_fusion.2.refs_1_), channel_id=1, source_target_pairs={{0,1},{1,0},{2,3},{3,2},{4,6},{5,7},{6,4},{7,5},{8,9},{9,8},{10,11... | collective-permute-start | bytes 786440 | tf_op jit(solution)/shard_map/ppermute | solution.py:24
  19.5 11.0 %collective-permute-start.9 = (bf16[4,32,1024]{2,1,0:T(8,128)(2,1)S(1)}, bf16[4,32,1024]{2,1,0:T(8,128)(2,1)S(1)}, u32[]{:S(2)}, u32[]{:S(2)}) collective-permute-start(bf16[4,32,1024]{2,1,0:T(8,128)(2,1)S(1)} %pad_maximum_fusion.2.refs_1_), channel_id=1, source_target_pairs={{0,4},{1,5},{2,6},{3,7},{4,0},{5,1},{6,2},{7,3},{8,12},{9,13},{10,... | collective-permute-start | bytes 786440 | tf_op jit(solution)/shard_map/ppermute | solution.py:24
  19.5 10.9 %copy-start.8 = (bf16[128,1024]{1,0:T(8,128)(2,1)}, bf16[128,1024]{1,0:T(8,128)(2,1)S(1)}, u32[]{:S(2)}) copy-start(bf16[128,1024]{1,0:T(8,128)(2,1)S(1)} %collective-permute-done.17) | copy-start | bytes 786436
  19.6 13.1 %collective-permute-start.7 = (bf16[4,32,1024]{2,1,0:T(8,128)(2,1)S(1)}, bf16[4,32,1024]{2,1,0:T(8,128)(2,1)}, u32[]{:S(2)}, u32[]{:S(2)}) collective-permute-start(bf16[4,32,1024]{2,1,0:T(8,128)(2,1)S(1)} %pad_maximum_fusion.2.refs_1_), channel_id=1, source_target_pairs={{0,2},{1,3},{2,0},{3,1},{4,5},{5,4},{6,7},{7,6},{8,10},{9,11},{10,... | collective-permute-start | bytes 786440 | tf_op jit(solution)/shard_map/ppermute | solution.py:24
  22.7 13.7 %collective-permute-start.15 = (bf16[256,512]{1,0:T(8,128)(2,1)S(1)}, bf16[256,512]{1,0:T(8,128)(2,1)}, u32[]{:S(2)}, u32[]{:S(2)}) collective-permute-start(bf16[256,512]{1,0:T(8,128)(2,1)S(1)} %get-tuple-element.13.refs_9_), channel_id=1, source_target_pairs={{0,16},{1,17},{2,18},{3,19},{4,20},{5,21},{6,22},{7,23},{8,24},{9,... | collective-permute-start | bytes 786440 | tf_op jit(solution)/shard_map/ppermute | solution.py:24
  26.4 4.1 %copy-start.2 = (bf16[4,32,1024]{2,1,0:T(8,128)(2,1)}, bf16[4,32,1024]{2,1,0:T(8,128)(2,1)S(1)}, u32[]{:S(2)}) copy-start(bf16[4,32,1024]{2,1,0:T(8,128)(2,1)S(1)} %collective-permute-done.21.refs_2_) | copy-start | bytes 786436
  26.4 11.6 %collective-permute-start.14 = (bf16[256,512]{1,0:T(8,128)(2,1)S(1)}, bf16[256,512]{1,0:T(8,128)(2,1)S(1)}, u32[]{:S(2)}, u32[]{:S(2)}) collective-permute-start(bf16[256,512]{1,0:T(8,128)(2,1)S(1)} %get-tuple-element.13.refs_9_), channel_id=1, source_target_pairs={{0,8},{1,9},{2,10},{3,11},{4,12},{5,13},{6,14},{7,15},{8,0},{9,1},... | collective-permute-start | bytes 786440 | tf_op jit(solution)/shard_map/ppermute | solution.py:24
  28.8 10.3 %collective-permute-start.8 = (bf16[4,32,1024]{2,1,0:T(8,128)(2,1)}, bf16[4,32,1024]{2,1,0:T(8,128)(2,1)}, u32[]{:S(2)}, u32[]{:S(2)}) collective-permute-start(bf16[4,32,1024]{2,1,0:T(8,128)(2,1)} %collective-permute-done.6.refs_2_), channel_id=1, source_target_pairs={{0,2},{1,3},{2,0},{3,1},{4,5},{5,4},{6,7},{7,6},{8,10},{9,11},{10,... | collective-permute-start | bytes 786440 | tf_op jit(solution)/shard_map/ppermute | solution.py:24
  30.5 0.7 copy-start.4
  31.2 38.9 %collective-permute-start = (bf16[1024,512]{1,0:T(8,128)(2,1)S(1)}, bf16[1024,512]{1,0:T(8,128)(2,1)S(1)}, u32[]{:S(2)}, u32[]{:S(2)}) collective-permute-start(bf16[1024,512]{1,0:T(8,128)(2,1)S(1)} %copy-done.1), channel_id=1, source_target_pairs={{0,1},{1,0},{2,3},{3,2},{4,6},{5,7},{6,4},{7,5},{8,9},{9,8},{10,11... | collective-permute-start | bytes 3145736 | tf_op jit(solution)/shard_map/ppermute | solution.py:24
  32.7 7.6 %collective-permute-start.11 = (bf16[4,32,1024]{2,1,0:T(8,128)(2,1)}, bf16[4,32,1024]{2,1,0:T(8,128)(2,1)}, u32[]{:S(2)}, u32[]{:S(2)}) collective-permute-start(bf16[4,32,1024]{2,1,0:T(8,128)(2,1)} %collective-permute-done.7.refs_3_), channel_id=1, source_target_pairs={{0,4},{1,5},{2,6},{3,7},{4,0},{5,1},{6,2},{7,3},{8,12},{9,13},{10,... | collective-permute-start | bytes 786440 | tf_op jit(solution)/shard_map/ppermute | solution.py:24
  36.4 4.4 %collective-permute-start.10 = (bf16[4,32,1024]{2,1,0:T(8,128)(2,1)}, bf16[4,32,1024]{2,1,0:T(8,128)(2,1)}, u32[]{:S(2)}, u32[]{:S(2)}) collective-permute-start(bf16[4,32,1024]{2,1,0:T(8,128)(2,1)} %collective-permute-done.6.refs_2_), channel_id=1, source_target_pairs={{0,4},{1,5},{2,6},{3,7},{4,0},{5,1},{6,2},{7,3},{8,12},{9,13},{10,... | collective-permute-start | bytes 786440 | tf_op jit(solution)/shard_map/ppermute | solution.py:24
  38.0 0.7 copy-start.6
  38.7 7.5 %collective-permute-start.16 = (bf16[256,512]{1,0:T(8,128)(2,1)}, bf16[256,512]{1,0:T(8,128)(2,1)}, u32[]{:S(2)}, u32[]{:S(2)}) collective-permute-start(bf16[256,512]{1,0:T(8,128)(2,1)} %collective-permute-done.15.refs_11_), channel_id=1, source_target_pairs={{0,8},{1,9},{2,10},{3,11},{4,12},{5,13},{6,14},{7,15},{8,0},{9,1},... | collective-permute-start | bytes 786440 | tf_op jit(solution)/shard_map/ppermute | solution.py:24
  39.1 7.1 %collective-permute-start.12 = (bf16[4,32,1024]{2,1,0:T(8,128)(2,1)}, bf16[4,32,1024]{2,1,0:T(8,128)(2,1)}, u32[]{:S(2)}, u32[]{:S(2)}) collective-permute-start(bf16[4,32,1024]{2,1,0:T(8,128)(2,1)} %collective-permute-done.8.refs_4_), channel_id=1, source_target_pairs={{0,4},{1,5},{2,6},{3,7},{4,0},{5,1},{6,2},{7,3},{8,12},{9,13},{10,... | collective-permute-start | bytes 786440 | tf_op jit(solution)/shard_map/ppermute | solution.py:24
  40.3 14.9 %copy-start.3 = (bf16[4,32,1024]{2,1,0:T(8,128)(2,1)S(1)}, bf16[4,32,1024]{2,1,0:T(8,128)(2,1)}, u32[]{:S(2)}) copy-start(bf16[4,32,1024]{2,1,0:T(8,128)(2,1)} %copy-done.2) | copy-start | bytes 786436
  40.3 14.9 %collective-permute-start.24 = (bf16[4,32,1024]{2,1,0:T(8,128)(2,1)S(1)}, bf16[4,32,1024]{2,1,0:T(8,128)(2,1)S(1)}, u32[]{:S(2)}, u32[]{:S(2)}) collective-permute-start(bf16[4,32,1024]{2,1,0:T(8,128)(2,1)S(1)} %pad_maximum_fusion.3.refs_1_), channel_id=1, source_target_pairs={{0,4},{1,5},{2,6},{3,7},{4,0},{5,1},{6,2},{7,3},{8,12},{9,13},{10,... | collective-permute-start | bytes 786440 | tf_op jit(solution)/shard_map/ppermute | solution.py:24
  40.9 14.6 %collective-permute-start.23 = (bf16[4,32,1024]{2,1,0:T(8,128)(2,1)}, bf16[4,32,1024]{2,1,0:T(8,128)(2,1)S(1)}, u32[]{:S(2)}, u32[]{:S(2)}) collective-permute-start(bf16[4,32,1024]{2,1,0:T(8,128)(2,1)} %copy-done.2), channel_id=1, source_target_pairs={{0,2},{1,3},{2,0},{3,1},{4,5},{5,4},{6,7},{7,6},{8,10},{9,11},{10,... | collective-permute-start | bytes 786440 | tf_op jit(solution)/shard_map/ppermute | solution.py:24
  46.2 9.6 %collective-permute-start.26 = (bf16[4,32,1024]{2,1,0:T(8,128)(2,1)S(1)}, bf16[4,32,1024]{2,1,0:T(8,128)(2,1)S(1)}, u32[]{:S(2)}, u32[]{:S(2)}) collective-permute-start(bf16[4,32,1024]{2,1,0:T(8,128)(2,1)S(1)} %collective-permute-done.22.refs_3_), channel_id=1, source_target_pairs={{0,4},{1,5},{2,6},{3,7},{4,0},{5,1},{6,2},{7,3},{8,12},{9,13},{10,... | collective-permute-start | bytes 786440 | tf_op jit(solution)/shard_map/ppermute | solution.py:24
  46.2 1.0 copy-start.5
  47.2 0.9 copy-start.7
  52.9 15.4 %collective-permute-start.29 = (bf16[256,512]{1,0:T(8,128)(2,1)S(1)}, bf16[256,512]{1,0:T(8,128)(2,1)S(1)}, u32[]{:S(2)}, u32[]{:S(2)}) collective-permute-start(bf16[256,512]{1,0:T(8,128)(2,1)S(1)} %get-tuple-element.7.refs_9_), channel_id=1, source_target_pairs={{0,16},{1,17},{2,18},{3,19},{4,20},{5,21},{6,22},{7,23},{8,24},{9,... | collective-permute-start | bytes 786440 | tf_op jit(solution)/shard_map/ppermute | solution.py:24
  55.2 13.3 %collective-permute-start.25 = (bf16[4,32,1024]{2,1,0:T(8,128)(2,1)S(1)}, bf16[4,32,1024]{2,1,0:T(8,128)(2,1)S(1)}, u32[]{:S(2)}, u32[]{:S(2)}) collective-permute-start(bf16[4,32,1024]{2,1,0:T(8,128)(2,1)S(1)} %copy-done.3), channel_id=1, source_target_pairs={{0,4},{1,5},{2,6},{3,7},{4,0},{5,1},{6,2},{7,3},{8,12},{9,13},{10,... | collective-permute-start | bytes 786440 | tf_op jit(solution)/shard_map/ppermute | solution.py:24
  55.5 14.6 %collective-permute-start.27 = (bf16[4,32,1024]{2,1,0:T(8,128)(2,1)S(1)}, bf16[4,32,1024]{2,1,0:T(8,128)(2,1)S(1)}, u32[]{:S(2)}, u32[]{:S(2)}) collective-permute-start(bf16[4,32,1024]{2,1,0:T(8,128)(2,1)S(1)} %collective-permute-done.23.refs_4_), channel_id=1, source_target_pairs={{0,4},{1,5},{2,6},{3,7},{4,0},{5,1},{6,2},{7,3},{8,12},{9,13},{10,... | collective-permute-start | bytes 786440 | tf_op jit(solution)/shard_map/ppermute | solution.py:24
  55.7 15.7 %collective-permute-start.28 = (bf16[256,512]{1,0:T(8,128)(2,1)S(1)}, bf16[256,512]{1,0:T(8,128)(2,1)S(1)}, u32[]{:S(2)}, u32[]{:S(2)}) collective-permute-start(bf16[256,512]{1,0:T(8,128)(2,1)S(1)} %get-tuple-element.7.refs_9_), channel_id=1, source_target_pairs={{0,8},{1,9},{2,10},{3,11},{4,12},{5,13},{6,14},{7,15},{8,0},{9,1},... | collective-permute-start | bytes 786440 | tf_op jit(solution)/shard_map/ppermute | solution.py:24
  68.3 7.9 %collective-permute-start.30 = (bf16[256,512]{1,0:T(8,128)(2,1)S(1)}, bf16[256,512]{1,0:T(8,128)(2,1)S(1)}, u32[]{:S(2)}, u32[]{:S(2)}) collective-permute-start(bf16[256,512]{1,0:T(8,128)(2,1)S(1)} %collective-permute-done.29.refs_11_), channel_id=1, source_target_pairs={{0,8},{1,9},{2,10},{3,11},{4,12},{5,13},{6,14},{7,15},{8,0},{9,1},... | collective-permute-start | bytes 786440 | tf_op jit(solution)/shard_map/ppermute | solution.py:24
  68.6 14.8 %collective-permute-start.1 = (bf16[1024,512]{1,0:T(8,128)(2,1)S(1)}, bf16[1024,512]{1,0:T(8,128)(2,1)S(1)}, u32[]{:S(2)}, u32[]{:S(2)}) collective-permute-start(bf16[1024,512]{1,0:T(8,128)(2,1)S(1)} %copy-done.1), channel_id=1, source_target_pairs={{0,2},{1,3},{2,0},{3,1},{4,5},{5,4},{6,7},{7,6},{8,10},{9,11},{10,... | collective-permute-start | bytes 3145736 | tf_op jit(solution)/shard_map/ppermute | solution.py:24
  70.1 24.5 %copy-start = (bf16[1024,1024]{1,0:T(8,128)(2,1)S(1)}, bf16[1024,1024]{1,0:T(8,128)(2,1)}, u32[]{:S(2)}) copy-start(bf16[1024,1024]{1,0:T(8,128)(2,1)} %refs_8_.1) | copy-start | bytes 6291460
  70.1 13.3 %collective-permute-start.31 = (bf16[1024,512]{1,0:T(8,128)(2,1)S(1)}, bf16[1024,512]{1,0:T(8,128)(2,1)S(1)}, u32[]{:S(2)}, u32[]{:S(2)}) collective-permute-start(bf16[1024,512]{1,0:T(8,128)(2,1)S(1)} %get-tuple-element.6.refs_4_), channel_id=1, source_target_pairs={{0,4},{1,5},{2,6},{3,7},{4,0},{5,1},{6,2},{7,3},{8,12},{9,13},{10,... | collective-permute-start | bytes 3145736 | tf_op jit(solution)/shard_map/ppermute | solution.py:24
  70.1 24.5 %collective-permute-start.2 = (bf16[1024,512]{1,0:T(8,128)(2,1)S(1)}, bf16[1024,512]{1,0:T(8,128)(2,1)S(1)}, u32[]{:S(2)}, u32[]{:S(2)}) collective-permute-start(bf16[1024,512]{1,0:T(8,128)(2,1)S(1)} %collective-permute-done.refs_1_), channel_id=1, source_target_pairs={{0,2},{1,3},{2,0},{3,1},{4,5},{5,4},{6,7},{7,6},{8,10},{9,11},{10,... | collective-permute-start | bytes 3145736 | tf_op jit(solution)/shard_map/ppermute | solution.py:24
  82.8 11.8 %collective-permute-start.32 = (bf16[1024,512]{1,0:T(8,128)(2,1)S(1)}, bf16[1024,512]{1,0:T(8,128)(2,1)S(1)}, u32[]{:S(2)}, u32[]{:S(2)}) collective-permute-start(bf16[1024,512]{1,0:T(8,128)(2,1)S(1)} %shard_map.69.refs_5_), channel_id=1, source_target_pairs={{0,4},{1,5},{2,6},{3,7},{4,0},{5,1},{6,2},{7,3},{8,12},{9,13},{10,... | collective-permute-start | bytes 3145736 | tf_op jit(solution)/shard_map/ppermute | solution.py:24

commit v2 on v0

v2 whole, which is shorter than its diff:
```python
import functools

import jax
import jax.numpy as jnp
from jax import lax
from jax.experimental import pallas as pl
from jax.experimental.pallas import tpu as pltpu
from jax.sharding import PartitionSpec as P

VMEM_BYTES = 40 * 1024 * 1024

CHUNKS = 1


def bits_of(size):
    return [1 << b for b in reversed(range(size.bit_length() - 1))]


def send(x, sizes, to):
    rows, cols = sizes
    pairs = []
    for r in range(rows):
        for c in range(cols):
            there_r, there_c = to(r, c)
            pairs.append((r * cols + c, there_r * cols + there_c))
    return lax.ppermute(x, ("row", "col"), pairs)


def after(x, *done):
    return lax.optimization_barrier((x, done))[0]


def plane_bits(cols, core):
    bits = bits_of(cols)
    return bits[::-1] if core == 0 else bits


def plane_owner(c, m, cols, core):
    offsets = []
    for which in (0, 1):
        bits = plane_bits(cols, which)
        offsets.append(sum(bit for i, bit in enumerate(bits) if m >> i & 1))
    return c ^ jnp.where(core == 0, offsets[0], offsets[1])


def product(left, right):
    return jnp.dot(left, right, preferred_element_type=jnp.float32)


def cost_of(us):
    return pl.CostEstimate(flops=us * 10**9, transcendentals=0, bytes_accessed=0) if us else None


def call(kernel, out_shape, place, *operands, scratch_shapes=(), cost=None, outputs=pltpu.VMEM):
    vmem = pl.BlockSpec(memory_space=pltpu.VMEM)
    return pl.pallas_call(
        kernel,
        out_shape=out_shape,
        in_specs=[pl.BlockSpec(memory_space=pltpu.SMEM)] + [vmem] * len(operands),
        out_specs=jax.tree.map(lambda _: pl.BlockSpec(memory_space=outputs), out_shape),
        scratch_shapes=scratch_shapes,
        cost_estimate=cost,
        compiler_params=pltpu.CompilerParams(vmem_limit_bytes=VMEM_BYTES),
    )(place, *operands)


def tri_at(z, wide):
    return wide * (z * (z + 1) // 2)


def pack_kernel(place_ref, *refs):
    pieces, out_ref = refs[:-1], refs[-1]
    chips, wide = len(pieces), pieces[0].shape[1] // len(pieces)
    height = out_ref.shape[0]
    for s in range(chips):
        for owner in range(chips):

            @pl.when(place_ref[0] ^ s == owner)
            def _(s=s, owner=owner):
                depth = wide * (owner + 1)
                for panel in range(2):
                    left = panel * tri_at(chips, wide) + tri_at(owner, wide)
                    rows = slice(panel * height, (panel + 1) * height)
                    out_ref[:, left : left + depth] = pieces[s][rows, :depth]


def pack_rows(place, pieces, cost):
    height, pb = pieces[0].shape[0] // 2, pieces[0].shape[1]
    width = 2 * tri_at(len(pieces), pb // len(pieces))
    out_shape = jax.ShapeDtypeStruct((height, width), jnp.bfloat16)
    return call(pack_kernel, out_shape, place, *pieces, cost=cost_of(cost))


def unpack_kernel(chips, rows_dev, place_ref, *refs):
    packs, out_ref = refs[:-1], refs[-1]
    cols = len(packs) // 2
    k, c = place_ref[1], place_ref[2]
    height, wide = packs[0].shape[0], out_ref.shape[2] // chips
    for at, pack in enumerate(packs):
        core = k if at < cols else 1 - k
        row = core * rows_dev + plane_owner(c, at % cols, cols, core) * height
        for z in range(chips):
            rows = pl.ds(pl.multiple_of(z * 2 * rows_dev + row, height), height)
            for panel in range(2):
                left, depth = panel * tri_at(chips, wide) + tri_at(z, wide), wide * (z + 1)
                out_ref[panel, rows, :depth] = pack[:, left : left + depth]


def unpack_rows(place, packs, chips, rows_dev, pb):
    out_shape = jax.ShapeDtypeStruct((2, pb, pb), jnp.bfloat16)
    return call(functools.partial(unpack_kernel, chips, rows_dev), out_shape, place, *packs)


def lower_product(place_ref, inverse, blocks, out_ref, right):
    z, k = place_ref[0], place_ref[1]
    rows_dev = blocks[0].shape[0] // 2
    for s, block in enumerate(blocks):
        for part, core in ((0, k), (1, 1 - k)):
            row = pl.multiple_of((z ^ s) * 2 * rows_dev + core * rows_dev, rows_dev)
            right[pl.ds(row, rows_dev), :] = block[part * rows_dev : (part + 1) * rows_dev, :]
    step = 2 * rows_dev
    for top in range(0, right.shape[0], step):
        out_ref[top : top + step, :] = product(
            inverse[top : top + step, : top + step], right[: top + step, :]
        ).astype(out_ref.dtype)


def first_kernel(place_ref, inverse, mine, theirs, below, *refs):
    blocks, (first, *carried, right) = refs[: -2 - CHUNKS], refs[-2 - CHUNKS :]
    lower_product(place_ref, inverse.at[0], blocks, first, right)
    width = carried[0].shape[1]
    rows_dev = mine.shape[0]
    for part, coupling in enumerate((mine, theirs)):
        rows = slice(part * rows_dev, (part + 1) * rows_dev)
        new = below[rows, :].astype(jnp.float32) - product(coupling[...], first[...])
        for chunk, out in enumerate(carried):
            out[rows, :] = new[:, chunk * width : (chunk + 1) * width].astype(out.dtype)


def second_kernel(place_ref, inverse, *refs):
    blocks, (second, right) = refs[:-2], refs[-2:]
    lower_product(place_ref, inverse.at[1], blocks, second, right)


def trailing_rows(panel, place_ref, total, factors, mine, theirs, out, done=None):
    k, c = place_ref[1], place_ref[2]
    cols = len(factors)
    depth, width = factors[0].shape[1], out.shape[1] // 2
    step, wide = min(256, out.shape[0]), mine[0].shape[1]
    for which in (0, 1):
        for upper in (0, 1):

            @pl.when(jnp.logical_and(k == which, c // (cols // 2) == upper))
            def _(which=which, upper=upper):
                at = plane_bits(cols, which).index(cols // 2)
                held = [m for m in range(cols) if m >> at & 1 == upper ^ panel]
                tops = [plane_owner(c, m, cols, which) % (cols // 2) * depth for m in held]
                tops = [pl.multiple_of(top, depth) for top in tops]
                for top in range(0, out.shape[0], step):
                    rows = slice(top, top + step)
                    left = jnp.concatenate([factors[m][rows, :] for m in held], axis=1)
                    for x, core in ((mine, which), (theirs, 1 - which)):
                        for chunk, part in enumerate(x):
                            right = [part[pl.ds(row, depth), :] for row in tops]
                            left_at = core * width + chunk * wide
                            columns = slice(left_at, left_at + wide)
                            out[rows, columns] = (
                                total[rows, columns].astype(jnp.float32)
                                - product(left, jnp.concatenate(right, axis=0))
                            ).astype(out.dtype)
                    if done:
                        done(rows)


def total_kernel(place_ref, rhs, *refs):
    factors, (mine, theirs, total) = refs[:-3], refs[-3:]
    trailing_rows(0, place_ref, rhs, factors, [mine], [theirs], total)


def last_kernel(place_ref, total, first, first_theirs, *refs):
    updated, solved, new_rows, new_solved, row_sems, solved_sem = refs[-6:]
    factors, x = refs[: -6 - 2 * CHUNKS], refs[-6 - 2 * CHUNKS : -6]
    second, second_theirs = x[:CHUNKS], x[CHUNKS:]
    z, k = place_ref[0], place_ref[1]
    rows_dev, width = solved.shape[1], first.shape[1]
    own = pl.ds(pl.multiple_of((2 * z + k) * rows_dev, rows_dev), rows_dev)
    panels = (([first], [first_theirs]), (second, second_theirs))
    for panel, halves in enumerate(panels):
        for half, core in zip(halves, (k, 1 - k)):
            wide = half[0].shape[1]
            for chunk, part in enumerate(half):
                left = pl.multiple_of(core * width + chunk * wide, wide)
                new_solved[panel, :, pl.ds(left, wide)] = part[own, :]
    store_solved = pltpu.make_async_copy(new_solved, solved, solved_sem)
    store_solved.start()
    step = updated.shape[0] // row_sems.shape[0]

    def store(rows):
        return pltpu.make_async_copy(
            new_rows.at[rows], updated.at[rows], row_sems.at[rows.start // step]
        )

    def done(rows):
        store(rows).start()

    trailing_rows(1, place_ref, total, factors, second, second_theirs, new_rows, done)
    for top in range(0, updated.shape[0], step):
        store(slice(top, top + step)).wait()
    store_solved.wait()


def by_permutes(sizes, rhs_top, diag_inverse, panel_coupling, trailing_factor, rhs_trailing):
    rows, cols = sizes
    chips = rows // 2
    rows_dev, pb = diag_inverse.shape[1:]
    half = rhs_top.shape[2] // 2
    wide = half // CHUNKS
    height = rows_dev // cols
    r, c = lax.axis_index("row"), lax.axis_index("col")
    z, k = r // 2, r % 2
    place = jnp.stack([z, k, c]).astype(jnp.int32)
    far, near = bits_of(chips)

    def along(x, s):
        return send(x, sizes, lambda r, c: (r ^ (2 * s), c))

    def across(x, i):
        return send(x, sizes, lambda r, c: (r, c ^ plane_bits(cols, r % 2)[i]))

    def swap(x):
        return send(x, sizes, lambda r, c: (r ^ 1, c))

    def block(*shape, dtype=jnp.bfloat16):
        return jax.ShapeDtypeStruct(shape, dtype)

    def share_of(matrices):
        mine = lax.dynamic_slice_in_dim(matrices, c * height, height, 1)
        return mine.reshape(2 * height, pb)

    def columns(core):
        return lax.dynamic_slice_in_dim(rhs_top, core * half, half, 2)

    def first_and_carried(*args):
        return call(
            first_kernel,
            [block(pb, half)] + [block(2 * rows_dev, wide)] * CHUNKS,
            place,
            *args,
            scratch_shapes=[pltpu.VMEM((pb, half), jnp.bfloat16)],
            cost=cost_of(0),
        )

    def second_of(*args):
        scratch = [pltpu.VMEM((pb, wide), jnp.bfloat16)]
        return call(second_kernel, block(pb, wide), place, *args, scratch_shapes=scratch)

    def total_of(*args):
        out_shape = block(*rhs_trailing.shape, dtype=jnp.float32)
        return call(total_kernel, out_shape, place, rhs_trailing, *args, cost=cost_of(4))

    def outputs_of(*args):
        out_shape = [block(*rhs_trailing.shape), block(2, rows_dev, 2 * half)]
        n_stores = max(rhs_trailing.shape[0] // 256, 1)
        scratch = [pltpu.VMEM(out.shape, out.dtype) for out in out_shape]
        scratch += [pltpu.SemaphoreType.DMA((n_stores,)), pltpu.SemaphoreType.DMA]
        return call(last_kernel, out_shape, place, *args, scratch_shapes=scratch, outputs=pl.ANY)

    share = share_of(diag_inverse)
    share_far = along(share, far)
    share_near = along(share, near)
    share_last = along(after(share_far, share_near), near)
    pack = pack_rows(place, [share, share_near, share_far, share_last], 2)
    pack_a = across(pack, 0)
    pack_b = across(pack, 1)
    pack_theirs = swap(pack)
    pack_a_theirs = swap(pack_a)
    pack_b_theirs = swap(pack_b)
    swapped = swap(columns(1 - k))
    chip_rhs = jnp.concatenate([columns(k), swapped], axis=1)
    top_far = along(after(chip_rhs, share_far)[0], far)
    top_near = along(after(chip_rhs, share_last)[0], near)
    top_last = along(top_far, near)
    coupling_theirs = swap(after(panel_coupling, top_far))
    pack_ab = across(after(pack_a, (coupling_theirs, pack_b, top_near)), 1)
    pack_ab_theirs = swap(pack_ab)
    inverse = unpack_rows(
        place,
        [
            pack,
            pack_a,
            pack_b,
            pack_ab,
            pack_theirs,
            pack_a_theirs,
            pack_b_theirs,
            after(pack_ab_theirs,
            top_last),
        ],
        chips,
        rows_dev,
        pb,
    )
    first_carried = first_and_carried(
        inverse,
        panel_coupling,
        coupling_theirs,
        chip_rhs[1],
        chip_rhs[0],
        top_near,
        top_far,
        top_last,
    )
    first = first_carried[0]
    first_theirs = swap(after(first, top_last))
    carried_0 = first_carried[1]
    carried_far_0 = along(carried_0, far)
    carried_near_0 = along(carried_0, near)
    factor_a = across(after(trailing_factor, share), 0)
    factor_b = across(after(trailing_factor, (coupling_theirs, factor_a)), 1)
    carried_last_0 = along(after(carried_far_0, (carried_near_0, factor_b, first_theirs)), near)
    second_0 = second_of(inverse, carried_0, carried_near_0, carried_far_0, carried_last_0)
    second_0_theirs = swap(second_0)
    factor_ab = across(after(factor_a, (factor_b, pack_ab)), 1)
    total = total_of(trailing_factor, factor_a, factor_b, factor_ab, first, first_theirs)
    outputs = outputs_of(
        total,
        first,
        first_theirs,
        trailing_factor,
        factor_a,
        factor_b,
        factor_ab,
        second_0,
        second_0_theirs,
    )
    updated, solved = outputs
    return solved, updated


def by_gathers(rhs_top, diag_inverse, panel_coupling, trailing_factor, rhs_trailing):
    def whole(x):
        return lax.all_gather(x, "row", axis=0, tiled=True)

    first = product(diag_inverse[0], whole(rhs_top[0])).astype(jnp.bfloat16)
    first_all = whole(first)
    carried = rhs_top[1].astype(jnp.float32) - product(panel_coupling, first_all)
    second = product(diag_inverse[1], whole(carried.astype(jnp.bfloat16))).astype(jnp.bfloat16)
    x = jnp.concatenate([first_all, whole(second)], axis=0)
    factor = lax.all_gather(trailing_factor, "col", axis=1, tiled=True)
    updated = (rhs_trailing.astype(jnp.float32) - product(factor, x)).astype(jnp.bfloat16)
    return jnp.stack([first, second]), updated


def fits(sizes, rhs_top, diag_inverse):
    rows, cols = sizes
    whole_rows = diag_inverse.shape[1] % (16 * cols) == 0
    whole_columns = diag_inverse.shape[2] % (64 * rows) == 0 and rhs_top.shape[2] % 256 == 0
    return rows == 8 and cols == 4 and whole_rows and whole_columns


def solution(mesh):
    sizes = (mesh.shape["row"], mesh.shape["col"])

    def shards(rhs_top, diag_inverse, *others):
        if fits(sizes, rhs_top, diag_inverse):
            return by_permutes(sizes, rhs_top, diag_inverse, *others)
        return by_gathers(rhs_top, diag_inverse, *others)

    in_specs = (
        P(None, "row", "col"),
        P(None, "row", None),
        P("row", None),
        P("row", "col"),
        P("row", "col"),
    )
    out_specs = (P(None, "row", "col"), P("row", "col"))
    return jax.shard_map(shards, mesh=mesh, in_specs=in_specs, out_specs=out_specs, check_vma=False)
```

time: 207 us -> 77 us (0.37)
  waiting for transfers between devices: 169 us -> 36.4 us
  starting transfers between devices: 0.2 us -> 26.6 us
  matrix products: 16.9 us -> 0 us
  between operations: 13.8 us -> 0.99 us
  Pallas kernels: 0 us -> 11.4 us
  local copies, waits for them, and re-layouts: 6.89 us -> 1.2 us
    all_gather x5 -> x0, waiting for transfers between devices: 168 us -> none  [the longest x1 47.6 us: shards(): lax.all_gather(trailing_factor, 'col', axis=1, tiled=True)]
    ppermute x0 -> x23, waiting for transfers between devices: none -> 36.4 us  [send(): return lax.ppermute(x, ('row', 'col'), pairs)]
    ppermute x0 -> x23, starting transfers between devices: none -> 26.6 us  [send(): return lax.ppermute(x, ('row', 'col'), pairs)]
    dot_general x4 -> x0, matrix products: 16.9 us -> none  [the longest x1 8.6 us: shards(): jnp.dot(lax.all_gather(trailing_factor, 'col', axis=1, tiled=True), solut...]
    pallas_call x0 -> x6, Pallas kernels: none -> 11.4 us  [call(): pl.pallas_call(kernel, out_shape=out_shape, in_specs=[pl.BlockSpec(memory...]
    unnamed x14 -> x8, local copies, waits for them, and re-layouts: 5.16 us -> 0.03 us
  transfers between devices with their start and end apart: 5 -> 23, of which waited for: 5 -> 13; matrix products, arithmetic and copies ran while one was open for 3% -> 0% of each run, Pallas kernels for 0% -> 10%
where the time goes in v2:
time: 77 us; the launch traced here: 76.7 us
  waiting for transfers between devices  36.4 us (47%)
  starting transfers between devices  26.6 us (35%)
  Pallas kernels  11.4 us (15%)
  local copies, waits for them, and re-layouts  1.2 us (2%)
  between operations  0.99 us (1%)
    ppermute x23, waiting for transfers between devices, send(): return lax.ppermute(x, ('row', 'col'), pairs)  36.4 us
    ppermute x23, starting transfers between devices, send(): return lax.ppermute(x, ('row', 'col'), pairs)  26.6 us
    pallas_call x6, Pallas kernels, call(): pl.pallas_call(kernel, out_shape=out_shape, in_specs=[pl.BlockSpec(memory...  11.4 us
  transfers between devices with their start and end apart: 23, of which 13 were waited for; matrix products, arithmetic and copies ran while one was open for 0% of the time, Pallas kernels for 10%

profile of v2, /device:TPU:0, one launch (start us, length us, event | category | flops | bytes accessed | tf_op | source)
XLA Modules:
  0.0 76.7 jit_solution(5165307193352648126)
XLA Ops:
  0.6 0.0 copy-start
  0.7 1.1 %constant_dynamic-slice_fusion.1 = (bf16[2,128,512]{2,1,0:T(8,128)(2,1)S(1)}, bf16[2,128,512]{2,1,0:T(8,128)(2,1)S(1)}) fusion(bf16[2,128,1024]{2,1,0:T(8,128)(2,1)} %param.5, s32[]{:T(128)S(6)} %select_n.23, s32[]{:T(128)S(6)} %select_n.24), kind=kLoop, calls=%fused_computation.12 | loop fusion | bytes 1048584 | tf_op jit(solution)/shard_map/dynamic_slice | solution.py:241
  1.8 0.5 collective-permute-start.1
  2.3 0.0 copy-done
  2.3 2.7 %collective-permute-start.6 = (bf16[64,1024]{1,0:T(8,128)(2,1)S(1)}, bf16[64,1024]{1,0:T(8,128)(2,1)S(1)}, u32[]{:S(2)}, u32[]{:S(2)}) collective-permute-start(bf16[64,1024]{1,0:T(8,128)(2,1)S(1)} %bitcast.12), channel_id=1, source_target_pairs={{0,8},{1,9},{2,10},{3,11},{4,12},{5,13},{6,14},{7,15},{8,0},{9,1},... | collective-permute-start | bytes 393224 | tf_op jit(solution)/shard_map/ppermute | solution.py:26
  5.0 2.6 %collective-permute-start.2 = (bf16[64,1024]{1,0:T(8,128)(2,1)S(1)}, bf16[64,1024]{1,0:T(8,128)(2,1)S(1)}, u32[]{:S(2)}, u32[]{:S(2)}) collective-permute-start(bf16[64,1024]{1,0:T(8,128)(2,1)S(1)} %bitcast.13), channel_id=1, source_target_pairs={{0,16},{1,17},{2,18},{3,19},{4,20},{5,21},{6,22},{7,23},{8,24},{9,... | collective-permute-start | bytes 393224 | tf_op jit(solution)/shard_map/ppermute | solution.py:26
  7.6 1.5 %collective-permute-start = (bf16[1024,512]{1,0:T(8,128)(2,1)}, bf16[1024,512]{1,0:T(8,128)(2,1)S(1)}, u32[]{:S(2)}, u32[]{:S(2)}) collective-permute-start(bf16[1024,512]{1,0:T(8,128)(2,1)} %refs_0_.3), channel_id=1, source_target_pairs={{0,1},{1,0},{2,3},{3,2},{4,6},{5,7},{6,4},{7,5},{8,9},{9,8},{10,11... | collective-permute-start | bytes 3145736 | tf_op jit(solution)/shard_map/ppermute | solution.py:26
  9.1 0.1 pad_add_fusion.place_ref
  9.2 2.5 %collective-permute-done.6.refs_1_ = bf16[64,1024]{1,0:T(8,128)(2,1)S(1)} collective-permute-done((bf16[64,1024]{1,0:T(8,128)(2,1)S(1)}, bf16[64,1024]{1,0:T(8,128)(2,1)S(1)}, u32[]{:S(2)}, u32[]{:S(2)}) %collective-permute-start.6) | collective-permute-done | bytes 131104 | tf_op jit(solution)/shard_map/ppermute | solution.py:26
  11.7 2.6 %collective-permute-done.2.refs_2_ = bf16[64,1024]{1,0:T(8,128)(2,1)S(1)} collective-permute-done((bf16[64,1024]{1,0:T(8,128)(2,1)S(1)}, bf16[64,1024]{1,0:T(8,128)(2,1)S(1)}, u32[]{:S(2)}, u32[]{:S(2)}) %collective-permute-start.2) | collective-permute-done | bytes 131104 | tf_op jit(solution)/shard_map/ppermute | solution.py:26
  14.4 0.4 collective-permute-start.7
  14.8 0.0 collective-permute-done.1
  14.8 0.0 copy-start.2
  14.9 0.0 copy-start.1
  14.9 2.7 %collective-permute-start.3 = (bf16[256,512]{1,0:T(8,128)(2,1)S(1)}, bf16[256,512]{1,0:T(8,128)(2,1)S(1)}, u32[]{:S(2)}, u32[]{:S(2)}) collective-permute-start(bf16[256,512]{1,0:T(8,128)(2,1)S(1)} %slice_bitcast_fusion.1), channel_id=1, source_target_pairs={{0,16},{1,17},{2,18},{3,19},{4,20},{5,21},{6,22},{7,23},{8,24},{9,... | collective-permute-start | bytes 786440 | tf_op jit(solution)/shard_map/ppermute | solution.py:26
  17.5 3.8 %collective-permute-done.7.refs_3_ = bf16[64,1024]{1,0:T(8,128)(2,1)S(1)} collective-permute-done((bf16[64,1024]{1,0:T(8,128)(2,1)S(1)}, bf16[64,1024]{1,0:T(8,128)(2,1)S(1)}, u32[]{:S(2)}, u32[]{:S(2)}) %collective-permute-start.7) | collective-permute-done | bytes 131104 | tf_op jit(solution)/shard_map/ppermute | solution.py:26
  21.4 0.7 shard_map.68.refs_0_
  22.0 1.6 %collective-permute-start.9 = (bf16[32,5120]{1,0:T(8,128)(2,1)S(1)}, bf16[32,5120]{1,0:T(8,128)(2,1)S(1)}, u32[]{:S(2)}, u32[]{:S(2)}) collective-permute-start(bf16[32,5120]{1,0:T(8,128)(2,1)S(1)} %shard_map.68.refs_0_), channel_id=1, source_target_pairs={{0,2},{1,3},{2,0},{3,1},{4,5},{5,4},{6,7},{7,6},{8,10},{9,11},{10,... | collective-permute-start | bytes 983048 | tf_op jit(solution)/shard_map/ppermute | solution.py:26
  23.6 1.7 %collective-permute-start.8 = (bf16[32,5120]{1,0:T(8,128)(2,1)S(1)}, bf16[32,5120]{1,0:T(8,128)(2,1)S(1)}, u32[]{:S(2)}, u32[]{:S(2)}) collective-permute-start(bf16[32,5120]{1,0:T(8,128)(2,1)S(1)} %shard_map.68.refs_0_), channel_id=1, source_target_pairs={{0,1},{1,0},{2,3},{3,2},{4,6},{5,7},{6,4},{7,5},{8,9},{9,8},{10,11... | collective-permute-start | bytes 983048 | tf_op jit(solution)/shard_map/ppermute | solution.py:26
  25.4 0.1 collective-permute-start.10
  25.4 3.6 %collective-permute-done.3.refs_2_ = bf16[256,512]{1,0:T(8,128)(2,1)S(1)} collective-permute-done((bf16[256,512]{1,0:T(8,128)(2,1)S(1)}, bf16[256,512]{1,0:T(8,128)(2,1)S(1)}, u32[]{:S(2)}, u32[]{:S(2)}) %collective-permute-start.3) | collective-permute-done | bytes 262176 | tf_op jit(solution)/shard_map/ppermute | solution.py:26
  29.0 0.0 copy-done.2
  29.0 0.0 collective-permute-start.4
  29.0 2.8 %collective-permute-done.10.refs_1_ = bf16[256,512]{1,0:T(8,128)(2,1)S(1)} collective-permute-done((bf16[256,512]{1,0:T(8,128)(2,1)S(1)}, bf16[256,512]{1,0:T(8,128)(2,1)S(1)}, u32[]{:S(2)}, u32[]{:S(2)}) %collective-permute-start.10) | collective-permute-done | bytes 262176 | tf_op jit(solution)/shard_map/ppermute | solution.py:26
  31.9 0.0 collective-permute-done.9.refs_2_
  31.9 0.0 collective-permute-done.8.refs_1_
  31.9 0.0 collective-permute-done.4.theirs
  31.9 1.6 %collective-permute-start.11 = (bf16[32,5120]{1,0:T(8,128)(2,1)S(1)}, bf16[32,5120]{1,0:T(8,128)(2,1)S(1)}, u32[]{:S(2)}, u32[]{:S(2)}) collective-permute-start(bf16[32,5120]{1,0:T(8,128)(2,1)S(1)} %collective-permute-done.8.refs_1_), channel_id=1, source_target_pairs={{0,2},{1,3},{2,0},{3,1},{4,5},{5,4},{6,7},{7,6},{8,10},{9,11},{10,... | collective-permute-start | bytes 983048 | tf_op jit(solution)/shard_map/ppermute | solution.py:26
  33.4 0.0 collective-permute-start.17
  33.5 5.6 %collective-permute-done.11.refs_3_ = bf16[32,5120]{1,0:T(8,128)(2,1)S(1)} collective-permute-done((bf16[32,5120]{1,0:T(8,128)(2,1)S(1)}, bf16[32,5120]{1,0:T(8,128)(2,1)S(1)}, u32[]{:S(2)}, u32[]{:S(2)}) %collective-permute-start.11) | collective-permute-done | bytes 327712 | tf_op jit(solution)/shard_map/ppermute | solution.py:26
  39.0 0.0 collective-permute-start.16
  39.0 0.5 collective-permute-start.13
  39.5 0.0 collective-permute-start.15
  39.5 0.0 collective-permute-done.refs_1_
  39.5 0.5 collective-permute-start.14
  40.0 0.2 collective-permute-done.17.refs_3_
  40.2 0.0 copy-done.1
  40.2 1.5 %collective-permute-start.5 = (bf16[1024,512]{1,0:T(8,128)(2,1)S(1)}, bf16[1024,512]{1,0:T(8,128)(2,1)S(1)}, u32[]{:S(2)}, u32[]{:S(2)}) collective-permute-start(bf16[1024,512]{1,0:T(8,128)(2,1)S(1)} %copy-done.1), channel_id=1, source_target_pairs={{0,2},{1,3},{2,0},{3,1},{4,5},{5,4},{6,7},{7,6},{8,10},{9,11},{10,... | collective-permute-start | bytes 3145736 | tf_op jit(solution)/shard_map/ppermute | solution.py:26
  41.8 0.0 collective-permute-done.16.refs_7_
  41.8 0.0 collective-permute-done.13.refs_4_
  41.8 0.0 collective-permute-done.15.refs_6_
  41.8 0.2 collective-permute-done.14.refs_5_
  42.0 0.7 shard_map.69.inverse
  42.8 1.8 %shard_map.70 = (bf16[1024,512]{1,0:T(8,128)(2,1)S(1)}, bf16[256,512]{1,0:T(8,128)(2,1)S(1)}) custom-call(s32[3]{0:T(128)S(1)} %pad_add_fusion.place_ref, bf16[2,1024,1024]{2,1,0:T(8,128)(2,1)S(1)} %shard_map.69.inverse, bf16[128,1024]{1,0:T(8,128)(2,1)S(1)} %copy-done.2, bf16[128,1024]{1,0:T(8,128)(2,1)S(1)} %collective-permute-done.4.theirs, ...), custom_call_target="tpu_custom_call" | custom-call | tf_op jit(solution)/shard_map/pallas_call | solution.py:56
  44.6 0.0 copy-start.3
  44.6 0.2 collective-permute-start.18
  44.8 2.9 %collective-permute-start.20 = (bf16[256,512]{1,0:T(8,128)(2,1)S(1)}, bf16[256,512]{1,0:T(8,128)(2,1)S(1)}, u32[]{:S(2)}, u32[]{:S(2)}) collective-permute-start(bf16[256,512]{1,0:T(8,128)(2,1)S(1)} %get-tuple-element.28.refs_0_), channel_id=1, source_target_pairs={{0,16},{1,17},{2,18},{3,19},{4,20},{5,21},{6,22},{7,23},{8,24},{9,... | collective-permute-start | bytes 786440 | tf_op jit(solution)/shard_map/ppermute | solution.py:26
  47.7 2.5 %collective-permute-start.19 = (bf16[256,512]{1,0:T(8,128)(2,1)S(1)}, bf16[256,512]{1,0:T(8,128)(2,1)S(1)}, u32[]{:S(2)}, u32[]{:S(2)}) collective-permute-start(bf16[256,512]{1,0:T(8,128)(2,1)S(1)} %get-tuple-element.28.refs_0_), channel_id=1, source_target_pairs={{0,8},{1,9},{2,10},{3,11},{4,12},{5,13},{6,14},{7,15},{8,0},{9,1},... | collective-permute-start | bytes 786440 | tf_op jit(solution)/shard_map/ppermute | solution.py:26
  50.1 4.9 %collective-permute-done.5.refs_2_ = bf16[1024,512]{1,0:T(8,128)(2,1)S(1)} collective-permute-done((bf16[1024,512]{1,0:T(8,128)(2,1)S(1)}, bf16[1024,512]{1,0:T(8,128)(2,1)S(1)}, u32[]{:S(2)}, u32[]{:S(2)}) %collective-permute-start.5) | collective-permute-done | bytes 1048608 | tf_op jit(solution)/shard_map/ppermute | solution.py:26
  55.0 1.5 %collective-permute-start.12 = (bf16[1024,512]{1,0:T(8,128)(2,1)S(1)}, bf16[1024,512]{1,0:T(8,128)(2,1)S(1)}, u32[]{:S(2)}, u32[]{:S(2)}) collective-permute-start(bf16[1024,512]{1,0:T(8,128)(2,1)S(1)} %collective-permute-done.refs_1_), channel_id=1, source_target_pairs={{0,2},{1,3},{2,0},{3,1},{4,5},{5,4},{6,7},{7,6},{8,10},{9,11},{10,... | collective-permute-start | bytes 3145736 | tf_op jit(solution)/shard_map/ppermute | solution.py:26
  56.6 3.6 %collective-permute-done.20.refs_2_ = bf16[256,512]{1,0:T(8,128)(2,1)S(1)} collective-permute-done((bf16[256,512]{1,0:T(8,128)(2,1)S(1)}, bf16[256,512]{1,0:T(8,128)(2,1)S(1)}, u32[]{:S(2)}, u32[]{:S(2)}) %collective-permute-start.20) | collective-permute-done | bytes 262176 | tf_op jit(solution)/shard_map/ppermute | solution.py:26
  60.2 0.1 collective-permute-done.19.refs_1_
  60.3 0.0 collective-permute-done.18.refs_5_.first_theirs
  60.3 1.6 %collective-permute-start.21 = (bf16[256,512]{1,0:T(8,128)(2,1)S(1)}, bf16[256,512]{1,0:T(8,128)(2,1)S(1)}, u32[]{:S(2)}, u32[]{:S(2)}) collective-permute-start(bf16[256,512]{1,0:T(8,128)(2,1)S(1)} %collective-permute-done.20.refs_2_), channel_id=1, source_target_pairs={{0,8},{1,9},{2,10},{3,11},{4,12},{5,13},{6,14},{7,15},{8,0},{9,1},... | collective-permute-start | bytes 786440 | tf_op jit(solution)/shard_map/ppermute | solution.py:26
  61.9 6.3 %collective-permute-done.21.refs_3_ = bf16[256,512]{1,0:T(8,128)(2,1)S(1)} collective-permute-done((bf16[256,512]{1,0:T(8,128)(2,1)S(1)}, bf16[256,512]{1,0:T(8,128)(2,1)S(1)}, u32[]{:S(2)}, u32[]{:S(2)}) %collective-permute-start.21) | collective-permute-done | bytes 262176 | tf_op jit(solution)/shard_map/ppermute | solution.py:26
  68.2 1.5 %shard_map.72.refs_4_ = bf16[1024,512]{1,0:T(8,128)(2,1)S(1)} custom-call(s32[3]{0:T(128)S(1)} %pad_add_fusion.place_ref, bf16[2,1024,1024]{2,1,0:T(8,128)(2,1)S(1)} %shard_map.69.inverse, bf16[256,512]{1,0:T(8,128)(2,1)S(1)} %get-tuple-element.28.refs_0_, bf16[256,512]{1,0:T(8,128)(2,1)S(1)} %collective-permute-done.19.refs_1_, ...), custom_call_target="tpu_custom_call" | custom-call | tf_op jit(solution)/shard_map/pallas_call | solution.py:56
  69.7 0.1 collective-permute-start.22
  69.7 0.1 collective-permute-done.12.refs_3_
  69.8 0.0 copy-done.3
  69.8 2.9 %shard_map.71.total = f32[1024,1024]{1,0:T(8,128)S(1)} custom-call(s32[3]{0:T(128)S(1)} %pad_add_fusion.place_ref, bf16[1024,1024]{1,0:T(8,128)(2,1)S(1)} %copy-done.3, bf16[1024,512]{1,0:T(8,128)(2,1)S(1)} %copy-done.1, bf16[1024,512]{1,0:T(8,128)(2,1)S(1)} %collective-permute-done.refs_1_, bf16[1024,512]{1,0:T(8,128)(2,1)S(1)} %collective-permute-done.5.refs_2_, ...), custom_call_target="tpu_custom_call" | custom-call | flops 4000000000 | tf_op jit(solution)/shard_map/pallas_call | solution.py:56
  72.8 0.0 collective-permute-done.22.refs_5_
  72.8 3.8 %shard_map.73 = (bf16[1024,1024]{1,0:T(8,128)(2,1)}, bf16[2,128,1024]{2,1,0:T(8,128)(2,1)}) custom-call(s32[3]{0:T(128)S(1)} %pad_add_fusion.place_ref, f32[1024,1024]{1,0:T(8,128)S(1)} %shard_map.71.total, bf16[1024,512]{1,0:T(8,128)(2,1)S(1)} %get-tuple-element.27.refs_4_.first, bf16[1024,512]{1,0:T(8,128)(2,1)S(1)} %collective-permute-done.18.refs_5_.first_theirs, ...), custom_call_target="tpu_custom_call" | custom-call | tf_op jit(solution)/shard_map/pallas_call | solution.py:56
  (5 shorter events, 0.1 us)
Async XLA Ops:
  0.6 1.7 %copy-start = (bf16[2,128,1024]{2,1,0:T(8,128)(2,1)S(1)}, bf16[2,128,1024]{2,1,0:T(8,128)(2,1)}, u32[]{:S(2)}) copy-start(bf16[2,128,1024]{2,1,0:T(8,128)(2,1)} %param.6) | copy-start | bytes 1572868
  1.8 13.0 %collective-permute-start.1 = (bf16[2,128,512]{2,1,0:T(8,128)(2,1)S(1)}, bf16[2,128,512]{2,1,0:T(8,128)(2,1)S(1)}, u32[]{:S(2)}, u32[]{:S(2)}) collective-permute-start(bf16[2,128,512]{2,1,0:T(8,128)(2,1)S(1)} %get-tuple-element.35), channel_id=1, source_target_pairs={{0,4},{1,5},{2,6},{3,7},{4,0},{5,1},{6,2},{7,3},{8,12},{9,13},{10,... | collective-permute-start | bytes 786440 | tf_op jit(solution)/shard_map/ppermute | solution.py:26
  2.3 9.4 %collective-permute-start.6 = (bf16[64,1024]{1,0:T(8,128)(2,1)S(1)}, bf16[64,1024]{1,0:T(8,128)(2,1)S(1)}, u32[]{:S(2)}, u32[]{:S(2)}) collective-permute-start(bf16[64,1024]{1,0:T(8,128)(2,1)S(1)} %bitcast.12), channel_id=1, source_target_pairs={{0,8},{1,9},{2,10},{3,11},{4,12},{5,13},{6,14},{7,15},{8,0},{9,1},... | collective-permute-start | bytes 393224 | tf_op jit(solution)/shard_map/ppermute | solution.py:26
  5.0 9.4 %collective-permute-start.2 = (bf16[64,1024]{1,0:T(8,128)(2,1)S(1)}, bf16[64,1024]{1,0:T(8,128)(2,1)S(1)}, u32[]{:S(2)}, u32[]{:S(2)}) collective-permute-start(bf16[64,1024]{1,0:T(8,128)(2,1)S(1)} %bitcast.13), channel_id=1, source_target_pairs={{0,16},{1,17},{2,18},{3,19},{4,20},{5,21},{6,22},{7,23},{8,24},{9,... | collective-permute-start | bytes 393224 | tf_op jit(solution)/shard_map/ppermute | solution.py:26
  7.6 31.9 %collective-permute-start = (bf16[1024,512]{1,0:T(8,128)(2,1)}, bf16[1024,512]{1,0:T(8,128)(2,1)S(1)}, u32[]{:S(2)}, u32[]{:S(2)}) collective-permute-start(bf16[1024,512]{1,0:T(8,128)(2,1)} %refs_0_.3), channel_id=1, source_target_pairs={{0,1},{1,0},{2,3},{3,2},{4,6},{5,7},{6,4},{7,5},{8,9},{9,8},{10,11... | collective-permute-start | bytes 3145736 | tf_op jit(solution)/shard_map/ppermute | solution.py:26
  14.4 7.0 %collective-permute-start.7 = (bf16[64,1024]{1,0:T(8,128)(2,1)S(1)}, bf16[64,1024]{1,0:T(8,128)(2,1)S(1)}, u32[]{:S(2)}, u32[]{:S(2)}) collective-permute-start(bf16[64,1024]{1,0:T(8,128)(2,1)S(1)} %collective-permute-done.2.refs_2_), channel_id=1, source_target_pairs={{0,8},{1,9},{2,10},{3,11},{4,12},{5,13},{6,14},{7,15},{8,0},{9,1},... | collective-permute-start | bytes 393224 | tf_op jit(solution)/shard_map/ppermute | solution.py:26
  14.8 14.2 %copy-start.2 = (bf16[128,1024]{1,0:T(8,128)(2,1)S(1)}, bf16[128,1024]{1,0:T(8,128)(2,1)}, u32[]{:S(2)}) copy-start(bf16[128,1024]{1,0:T(8,128)(2,1)} %mine.1) | copy-start | bytes 786436
  14.9 25.4 %copy-start.1 = (bf16[1024,512]{1,0:T(8,128)(2,1)S(1)}, bf16[1024,512]{1,0:T(8,128)(2,1)}, u32[]{:S(2)}) copy-start(bf16[1024,512]{1,0:T(8,128)(2,1)} %refs_0_.3) | copy-start | bytes 3145732
  14.9 14.1 %collective-permute-start.3 = (bf16[256,512]{1,0:T(8,128)(2,1)S(1)}, bf16[256,512]{1,0:T(8,128)(2,1)S(1)}, u32[]{:S(2)}, u32[]{:S(2)}) collective-permute-start(bf16[256,512]{1,0:T(8,128)(2,1)S(1)} %slice_bitcast_fusion.1), channel_id=1, source_target_pairs={{0,16},{1,17},{2,18},{3,19},{4,20},{5,21},{6,22},{7,23},{8,24},{9,... | collective-permute-start | bytes 786440 | tf_op jit(solution)/shard_map/ppermute | solution.py:26
  22.0 9.8 %collective-permute-start.9 = (bf16[32,5120]{1,0:T(8,128)(2,1)S(1)}, bf16[32,5120]{1,0:T(8,128)(2,1)S(1)}, u32[]{:S(2)}, u32[]{:S(2)}) collective-permute-start(bf16[32,5120]{1,0:T(8,128)(2,1)S(1)} %shard_map.68.refs_0_), channel_id=1, source_target_pairs={{0,2},{1,3},{2,0},{3,1},{4,5},{5,4},{6,7},{7,6},{8,10},{9,11},{10,... | collective-permute-start | bytes 983048 | tf_op jit(solution)/shard_map/ppermute | solution.py:26
  23.6 8.2 %collective-permute-start.8 = (bf16[32,5120]{1,0:T(8,128)(2,1)S(1)}, bf16[32,5120]{1,0:T(8,128)(2,1)S(1)}, u32[]{:S(2)}, u32[]{:S(2)}) collective-permute-start(bf16[32,5120]{1,0:T(8,128)(2,1)S(1)} %shard_map.68.refs_0_), channel_id=1, source_target_pairs={{0,1},{1,0},{2,3},{3,2},{4,6},{5,7},{6,4},{7,5},{8,9},{9,8},{10,11... | collective-permute-start | bytes 983048 | tf_op jit(solution)/shard_map/ppermute | solution.py:26
  25.4 6.5 %collective-permute-start.10 = (bf16[256,512]{1,0:T(8,128)(2,1)S(1)}, bf16[256,512]{1,0:T(8,128)(2,1)S(1)}, u32[]{:S(2)}, u32[]{:S(2)}) collective-permute-start(bf16[256,512]{1,0:T(8,128)(2,1)S(1)} %slice_bitcast_fusion), channel_id=1, source_target_pairs={{0,8},{1,9},{2,10},{3,11},{4,12},{5,13},{6,14},{7,15},{8,0},{9,1},... | collective-permute-start | bytes 786440 | tf_op jit(solution)/shard_map/ppermute | solution.py:26
  29.0 2.8 %collective-permute-start.4 = (bf16[128,1024]{1,0:T(8,128)(2,1)S(1)}, bf16[128,1024]{1,0:T(8,128)(2,1)S(1)}, u32[]{:S(2)}, u32[]{:S(2)}) collective-permute-start(bf16[128,1024]{1,0:T(8,128)(2,1)S(1)} %copy-done.2), channel_id=1, source_target_pairs={{0,4},{1,5},{2,6},{3,7},{4,0},{5,1},{6,2},{7,3},{8,12},{9,13},{10,... | collective-permute-start | bytes 786440 | tf_op jit(solution)/shard_map/ppermute | solution.py:26
  31.9 7.1 %collective-permute-start.11 = (bf16[32,5120]{1,0:T(8,128)(2,1)S(1)}, bf16[32,5120]{1,0:T(8,128)(2,1)S(1)}, u32[]{:S(2)}, u32[]{:S(2)}) collective-permute-start(bf16[32,5120]{1,0:T(8,128)(2,1)S(1)} %collective-permute-done.8.refs_1_), channel_id=1, source_target_pairs={{0,2},{1,3},{2,0},{3,1},{4,5},{5,4},{6,7},{7,6},{8,10},{9,11},{10,... | collective-permute-start | bytes 983048 | tf_op jit(solution)/shard_map/ppermute | solution.py:26
  33.4 6.8 %collective-permute-start.17 = (bf16[256,512]{1,0:T(8,128)(2,1)S(1)}, bf16[256,512]{1,0:T(8,128)(2,1)S(1)}, u32[]{:S(2)}, u32[]{:S(2)}) collective-permute-start(bf16[256,512]{1,0:T(8,128)(2,1)S(1)} %collective-permute-done.3.refs_2_), channel_id=1, source_target_pairs={{0,8},{1,9},{2,10},{3,11},{4,12},{5,13},{6,14},{7,15},{8,0},{9,1},... | collective-permute-start | bytes 786440 | tf_op jit(solution)/shard_map/ppermute | solution.py:26
  39.0 2.8 %collective-permute-start.16 = (bf16[32,5120]{1,0:T(8,128)(2,1)S(1)}, bf16[32,5120]{1,0:T(8,128)(2,1)S(1)}, u32[]{:S(2)}, u32[]{:S(2)}) collective-permute-start(bf16[32,5120]{1,0:T(8,128)(2,1)S(1)} %collective-permute-done.11.refs_3_), channel_id=1, source_target_pairs={{0,4},{1,5},{2,6},{3,7},{4,0},{5,1},{6,2},{7,3},{8,12},{9,13},{10,... | collective-permute-start | bytes 983048 | tf_op jit(solution)/shard_map/ppermute | solution.py:26
  39.0 2.8 %collective-permute-start.13 = (bf16[32,5120]{1,0:T(8,128)(2,1)S(1)}, bf16[32,5120]{1,0:T(8,128)(2,1)S(1)}, u32[]{:S(2)}, u32[]{:S(2)}) collective-permute-start(bf16[32,5120]{1,0:T(8,128)(2,1)S(1)} %shard_map.68.refs_0_), channel_id=1, source_target_pairs={{0,4},{1,5},{2,6},{3,7},{4,0},{5,1},{6,2},{7,3},{8,12},{9,13},{10,... | collective-permute-start | bytes 983048 | tf_op jit(solution)/shard_map/ppermute | solution.py:26
  39.5 2.3 %collective-permute-start.15 = (bf16[32,5120]{1,0:T(8,128)(2,1)S(1)}, bf16[32,5120]{1,0:T(8,128)(2,1)S(1)}, u32[]{:S(2)}, u32[]{:S(2)}) collective-permute-start(bf16[32,5120]{1,0:T(8,128)(2,1)S(1)} %collective-permute-done.9.refs_2_), channel_id=1, source_target_pairs={{0,4},{1,5},{2,6},{3,7},{4,0},{5,1},{6,2},{7,3},{8,12},{9,13},{10,... | collective-permute-start | bytes 983048 | tf_op jit(solution)/shard_map/ppermute | solution.py:26
  39.5 2.5 %collective-permute-start.14 = (bf16[32,5120]{1,0:T(8,128)(2,1)S(1)}, bf16[32,5120]{1,0:T(8,128)(2,1)S(1)}, u32[]{:S(2)}, u32[]{:S(2)}) collective-permute-start(bf16[32,5120]{1,0:T(8,128)(2,1)S(1)} %collective-permute-done.8.refs_1_), channel_id=1, source_target_pairs={{0,4},{1,5},{2,6},{3,7},{4,0},{5,1},{6,2},{7,3},{8,12},{9,13},{10,... | collective-permute-start | bytes 983048 | tf_op jit(solution)/shard_map/ppermute | solution.py:26
  40.2 14.8 %collective-permute-start.5 = (bf16[1024,512]{1,0:T(8,128)(2,1)S(1)}, bf16[1024,512]{1,0:T(8,128)(2,1)S(1)}, u32[]{:S(2)}, u32[]{:S(2)}) collective-permute-start(bf16[1024,512]{1,0:T(8,128)(2,1)S(1)} %copy-done.1), channel_id=1, source_target_pairs={{0,2},{1,3},{2,0},{3,1},{4,5},{5,4},{6,7},{7,6},{8,10},{9,11},{10,... | collective-permute-start | bytes 3145736 | tf_op jit(solution)/shard_map/ppermute | solution.py:26
  44.6 25.3 %copy-start.3 = (bf16[1024,1024]{1,0:T(8,128)(2,1)S(1)}, bf16[1024,1024]{1,0:T(8,128)(2,1)}, u32[]{:S(2)}) copy-start(bf16[1024,1024]{1,0:T(8,128)(2,1)} %rhs.1) | copy-start | bytes 6291460
  44.6 15.7 %collective-permute-start.18 = (bf16[1024,512]{1,0:T(8,128)(2,1)S(1)}, bf16[1024,512]{1,0:T(8,128)(2,1)S(1)}, u32[]{:S(2)}, u32[]{:S(2)}) collective-permute-start(bf16[1024,512]{1,0:T(8,128)(2,1)S(1)} %get-tuple-element.27.refs_4_.first), channel_id=1, source_target_pairs={{0,4},{1,5},{2,6},{3,7},{4,0},{5,1},{6,2},{7,3},{8,12},{9,13},{10,... | collective-permute-start | bytes 3145736 | tf_op jit(solution)/shard_map/ppermute | solution.py:26
  44.8 15.4 %collective-permute-start.20 = (bf16[256,512]{1,0:T(8,128)(2,1)S(1)}, bf16[256,512]{1,0:T(8,128)(2,1)S(1)}, u32[]{:S(2)}, u32[]{:S(2)}) collective-permute-start(bf16[256,512]{1,0:T(8,128)(2,1)S(1)} %get-tuple-element.28.refs_0_), channel_id=1, source_target_pairs={{0,16},{1,17},{2,18},{3,19},{4,20},{5,21},{6,22},{7,23},{8,24},{9,... | collective-permute-start | bytes 786440 | tf_op jit(solution)/shard_map/ppermute | solution.py:26
  47.7 12.6 %collective-permute-start.19 = (bf16[256,512]{1,0:T(8,128)(2,1)S(1)}, bf16[256,512]{1,0:T(8,128)(2,1)S(1)}, u32[]{:S(2)}, u32[]{:S(2)}) collective-permute-start(bf16[256,512]{1,0:T(8,128)(2,1)S(1)} %get-tuple-element.28.refs_0_), channel_id=1, source_target_pairs={{0,8},{1,9},{2,10},{3,11},{4,12},{5,13},{6,14},{7,15},{8,0},{9,1},... | collective-permute-start | bytes 786440 | tf_op jit(solution)/shard_map/ppermute | solution.py:26
  55.0 14.8 %collective-permute-start.12 = (bf16[1024,512]{1,0:T(8,128)(2,1)S(1)}, bf16[1024,512]{1,0:T(8,128)(2,1)S(1)}, u32[]{:S(2)}, u32[]{:S(2)}) collective-permute-start(bf16[1024,512]{1,0:T(8,128)(2,1)S(1)} %collective-permute-done.refs_1_), channel_id=1, source_target_pairs={{0,2},{1,3},{2,0},{3,1},{4,5},{5,4},{6,7},{7,6},{8,10},{9,11},{10,... | collective-permute-start | bytes 3145736 | tf_op jit(solution)/shard_map/ppermute | solution.py:26
  60.3 7.9 %collective-permute-start.21 = (bf16[256,512]{1,0:T(8,128)(2,1)S(1)}, bf16[256,512]{1,0:T(8,128)(2,1)S(1)}, u32[]{:S(2)}, u32[]{:S(2)}) collective-permute-start(bf16[256,512]{1,0:T(8,128)(2,1)S(1)} %collective-permute-done.20.refs_2_), channel_id=1, source_target_pairs={{0,8},{1,9},{2,10},{3,11},{4,12},{5,13},{6,14},{7,15},{8,0},{9,1},... | collective-permute-start | bytes 786440 | tf_op jit(solution)/shard_map/ppermute | solution.py:26
  69.7 3.1 %collective-permute-start.22 = (bf16[1024,512]{1,0:T(8,128)(2,1)S(1)}, bf16[1024,512]{1,0:T(8,128)(2,1)S(1)}, u32[]{:S(2)}, u32[]{:S(2)}) collective-permute-start(bf16[1024,512]{1,0:T(8,128)(2,1)S(1)} %shard_map.72.refs_4_), channel_id=1, source_target_pairs={{0,4},{1,5},{2,6},{3,7},{4,0},{5,1},{6,2},{7,3},{8,12},{9,13},{10,... | collective-permute-start | bytes 3145736 | tf_op jit(solution)/shard_map/ppermute | solution.py:26

commit v3 on v2

--- a/solution.py
+++ b/solution.py
@@ -238,7 +238,7 @@
         return mine.reshape(2 * height, pb)
 
     def columns(core):
-        return lax.dynamic_slice_in_dim(rhs_top, core * half, half, 2)
+        return lax.dynamic_slice_in_dim(after(rhs_top, share), core * half, half, 2)
 
     def first_and_carried(*args):
         return call(

time: 77 us -> 77.9 us (1.012)
  local copies, waits for them, and re-layouts: 1.2 us -> 2.15 us
    unnamed x8, local copies, waits for them, and re-layouts: 0.03 us -> 1.03 us
where the time goes in v3:
time: 77.9 us; the launch traced here: 77.6 us
  waiting for transfers between devices  36.3 us (47%)
  starting transfers between devices  26.7 us (34%)
  Pallas kernels  11.4 us (15%)
  local copies, waits for them, and re-layouts  2.15 us (3%)
  between operations  0.99 us (1%)
    ppermute x23, waiting for transfers between devices, send(): return lax.ppermute(x, ('row', 'col'), pairs)  36.3 us
    ppermute x23, starting transfers between devices, send(): return lax.ppermute(x, ('row', 'col'), pairs)  26.7 us
    pallas_call x6, Pallas kernels, call(): pl.pallas_call(kernel, out_shape=out_shape, in_specs=[pl.BlockSpec(memory...  11.4 us
  transfers between devices with their start and end apart: 23, of which 13 were waited for; matrix products, arithmetic and copies ran while one was open for 0% of the time, Pallas kernels for 10%

profile of v3, /device:TPU:0, one launch (start us, length us, event | category | flops | bytes accessed | tf_op | source)
XLA Modules:
  0.0 77.6 jit_solution(11197849590363185896)
XLA Ops:
  0.6 0.0 copy-start
  0.7 1.0 %copy-done = bf16[2,128,1024]{2,1,0:T(8,128)(2,1)S(1)} copy-done((bf16[2,128,1024]{2,1,0:T(8,128)(2,1)S(1)}, bf16[2,128,1024]{2,1,0:T(8,128)(2,1)}, u32[]{:S(2)}) %copy-start) | copy-done | bytes 524312
  1.7 1.1 %constant_dynamic-slice_fusion.1 = (bf16[2,128,512]{2,1,0:T(8,128)(2,1)S(1)}, bf16[2,128,512]{2,1,0:T(8,128)(2,1)S(1)}) fusion(bf16[2,128,1024]{2,1,0:T(8,128)(2,1)} %param.5, s32[]{:T(128)S(6)} %select_n.23, s32[]{:T(128)S(6)} %select_n.24), kind=kLoop, calls=%fused_computation.12 | loop fusion | bytes 1048584 | tf_op jit(solution)/shard_map/dynamic_slice | solution.py:241
  2.8 0.5 collective-permute-start.1
  3.3 2.6 %collective-permute-start.6 = (bf16[64,1024]{1,0:T(8,128)(2,1)S(1)}, bf16[64,1024]{1,0:T(8,128)(2,1)S(1)}, u32[]{:S(2)}, u32[]{:S(2)}) collective-permute-start(bf16[64,1024]{1,0:T(8,128)(2,1)S(1)} %bitcast.12), channel_id=1, source_target_pairs={{0,8},{1,9},{2,10},{3,11},{4,12},{5,13},{6,14},{7,15},{8,0},{9,1},... | collective-permute-start | bytes 393224 | tf_op jit(solution)/shard_map/ppermute | solution.py:26
  5.9 2.6 %collective-permute-start.2 = (bf16[64,1024]{1,0:T(8,128)(2,1)S(1)}, bf16[64,1024]{1,0:T(8,128)(2,1)S(1)}, u32[]{:S(2)}, u32[]{:S(2)}) collective-permute-start(bf16[64,1024]{1,0:T(8,128)(2,1)S(1)} %bitcast.13), channel_id=1, source_target_pairs={{0,16},{1,17},{2,18},{3,19},{4,20},{5,21},{6,22},{7,23},{8,24},{9,... | collective-permute-start | bytes 393224 | tf_op jit(solution)/shard_map/ppermute | solution.py:26
  8.5 1.5 %collective-permute-start = (bf16[1024,512]{1,0:T(8,128)(2,1)}, bf16[1024,512]{1,0:T(8,128)(2,1)S(1)}, u32[]{:S(2)}, u32[]{:S(2)}) collective-permute-start(bf16[1024,512]{1,0:T(8,128)(2,1)} %refs_0_.3), channel_id=1, source_target_pairs={{0,1},{1,0},{2,3},{3,2},{4,6},{5,7},{6,4},{7,5},{8,9},{9,8},{10,11... | collective-permute-start | bytes 3145736 | tf_op jit(solution)/shard_map/ppermute | solution.py:26
  10.0 0.1 pad_add_fusion.place_ref
  10.1 2.5 %collective-permute-done.6.refs_1_ = bf16[64,1024]{1,0:T(8,128)(2,1)S(1)} collective-permute-done((bf16[64,1024]{1,0:T(8,128)(2,1)S(1)}, bf16[64,1024]{1,0:T(8,128)(2,1)S(1)}, u32[]{:S(2)}, u32[]{:S(2)}) %collective-permute-start.6) | collective-permute-done | bytes 131104 | tf_op jit(solution)/shard_map/ppermute | solution.py:26
  12.6 2.7 %collective-permute-done.2.refs_2_ = bf16[64,1024]{1,0:T(8,128)(2,1)S(1)} collective-permute-done((bf16[64,1024]{1,0:T(8,128)(2,1)S(1)}, bf16[64,1024]{1,0:T(8,128)(2,1)S(1)}, u32[]{:S(2)}, u32[]{:S(2)}) %collective-permute-start.2) | collective-permute-done | bytes 131104 | tf_op jit(solution)/shard_map/ppermute | solution.py:26
  15.3 0.4 collective-permute-start.7
  15.7 0.0 collective-permute-done.1
  15.8 0.0 copy-start.2
  15.8 0.0 copy-start.1
  15.8 2.7 %collective-permute-start.3 = (bf16[256,512]{1,0:T(8,128)(2,1)S(1)}, bf16[256,512]{1,0:T(8,128)(2,1)S(1)}, u32[]{:S(2)}, u32[]{:S(2)}) collective-permute-start(bf16[256,512]{1,0:T(8,128)(2,1)S(1)} %slice_bitcast_fusion.1), channel_id=1, source_target_pairs={{0,16},{1,17},{2,18},{3,19},{4,20},{5,21},{6,22},{7,23},{8,24},{9,... | collective-permute-start | bytes 786440 | tf_op jit(solution)/shard_map/ppermute | solution.py:26
  18.5 3.7 %collective-permute-done.7.refs_3_ = bf16[64,1024]{1,0:T(8,128)(2,1)S(1)} collective-permute-done((bf16[64,1024]{1,0:T(8,128)(2,1)S(1)}, bf16[64,1024]{1,0:T(8,128)(2,1)S(1)}, u32[]{:S(2)}, u32[]{:S(2)}) %collective-permute-start.7) | collective-permute-done | bytes 131104 | tf_op jit(solution)/shard_map/ppermute | solution.py:26
  22.1 0.7 shard_map.68.refs_0_
  22.8 1.6 %collective-permute-start.9 = (bf16[32,5120]{1,0:T(8,128)(2,1)S(1)}, bf16[32,5120]{1,0:T(8,128)(2,1)S(1)}, u32[]{:S(2)}, u32[]{:S(2)}) collective-permute-start(bf16[32,5120]{1,0:T(8,128)(2,1)S(1)} %shard_map.68.refs_0_), channel_id=1, source_target_pairs={{0,2},{1,3},{2,0},{3,1},{4,5},{5,4},{6,7},{7,6},{8,10},{9,11},{10,... | collective-permute-start | bytes 983048 | tf_op jit(solution)/shard_map/ppermute | solution.py:26
  24.4 1.8 %collective-permute-start.8 = (bf16[32,5120]{1,0:T(8,128)(2,1)S(1)}, bf16[32,5120]{1,0:T(8,128)(2,1)S(1)}, u32[]{:S(2)}, u32[]{:S(2)}) collective-permute-start(bf16[32,5120]{1,0:T(8,128)(2,1)S(1)} %shard_map.68.refs_0_), channel_id=1, source_target_pairs={{0,1},{1,0},{2,3},{3,2},{4,6},{5,7},{6,4},{7,5},{8,9},{9,8},{10,11... | collective-permute-start | bytes 983048 | tf_op jit(solution)/shard_map/ppermute | solution.py:26
  26.2 0.1 collective-permute-start.10
  26.3 3.6 %collective-permute-done.3.refs_2_ = bf16[256,512]{1,0:T(8,128)(2,1)S(1)} collective-permute-done((bf16[256,512]{1,0:T(8,128)(2,1)S(1)}, bf16[256,512]{1,0:T(8,128)(2,1)S(1)}, u32[]{:S(2)}, u32[]{:S(2)}) %collective-permute-start.3) | collective-permute-done | bytes 262176 | tf_op jit(solution)/shard_map/ppermute | solution.py:26
  29.9 0.0 copy-done.2
  29.9 0.0 collective-permute-start.4
  29.9 2.8 %collective-permute-done.10.refs_1_ = bf16[256,512]{1,0:T(8,128)(2,1)S(1)} collective-permute-done((bf16[256,512]{1,0:T(8,128)(2,1)S(1)}, bf16[256,512]{1,0:T(8,128)(2,1)S(1)}, u32[]{:S(2)}, u32[]{:S(2)}) %collective-permute-start.10) | collective-permute-done | bytes 262176 | tf_op jit(solution)/shard_map/ppermute | solution.py:26
  32.7 0.0 collective-permute-done.9.refs_2_
  32.7 0.0 collective-permute-done.8.refs_1_
  32.7 0.0 collective-permute-done.4.theirs
  32.7 1.6 %collective-permute-start.11 = (bf16[32,5120]{1,0:T(8,128)(2,1)S(1)}, bf16[32,5120]{1,0:T(8,128)(2,1)S(1)}, u32[]{:S(2)}, u32[]{:S(2)}) collective-permute-start(bf16[32,5120]{1,0:T(8,128)(2,1)S(1)} %collective-permute-done.8.refs_1_), channel_id=1, source_target_pairs={{0,2},{1,3},{2,0},{3,1},{4,5},{5,4},{6,7},{7,6},{8,10},{9,11},{10,... | collective-permute-start | bytes 983048 | tf_op jit(solution)/shard_map/ppermute | solution.py:26
  34.3 0.0 collective-permute-start.17
  34.3 5.6 %collective-permute-done.11.refs_3_ = bf16[32,5120]{1,0:T(8,128)(2,1)S(1)} collective-permute-done((bf16[32,5120]{1,0:T(8,128)(2,1)S(1)}, bf16[32,5120]{1,0:T(8,128)(2,1)S(1)}, u32[]{:S(2)}, u32[]{:S(2)}) %collective-permute-start.11) | collective-permute-done | bytes 327712 | tf_op jit(solution)/shard_map/ppermute | solution.py:26
  39.9 0.0 collective-permute-start.16
  39.9 0.5 collective-permute-start.13
  40.4 0.0 collective-permute-start.15
  40.4 0.0 collective-permute-done.refs_1_
  40.4 0.5 collective-permute-start.14
  40.9 0.2 collective-permute-done.17.refs_3_
  41.1 0.0 copy-done.1
  41.1 1.5 %collective-permute-start.5 = (bf16[1024,512]{1,0:T(8,128)(2,1)S(1)}, bf16[1024,512]{1,0:T(8,128)(2,1)S(1)}, u32[]{:S(2)}, u32[]{:S(2)}) collective-permute-start(bf16[1024,512]{1,0:T(8,128)(2,1)S(1)} %copy-done.1), channel_id=1, source_target_pairs={{0,2},{1,3},{2,0},{3,1},{4,5},{5,4},{6,7},{7,6},{8,10},{9,11},{10,... | collective-permute-start | bytes 3145736 | tf_op jit(solution)/shard_map/ppermute | solution.py:26
  42.7 0.0 collective-permute-done.16.refs_7_
  42.7 0.0 collective-permute-done.13.refs_4_
  42.7 0.0 collective-permute-done.15.refs_6_
  42.7 0.2 collective-permute-done.14.refs_5_
  42.9 0.7 shard_map.69.inverse
  43.7 1.8 %shard_map.70 = (bf16[1024,512]{1,0:T(8,128)(2,1)S(1)}, bf16[256,512]{1,0:T(8,128)(2,1)S(1)}) custom-call(s32[3]{0:T(128)S(1)} %pad_add_fusion.place_ref, bf16[2,1024,1024]{2,1,0:T(8,128)(2,1)S(1)} %shard_map.69.inverse, bf16[128,1024]{1,0:T(8,128)(2,1)S(1)} %copy-done.2, bf16[128,1024]{1,0:T(8,128)(2,1)S(1)} %collective-permute-done.4.theirs, ...), custom_call_target="tpu_custom_call" | custom-call | tf_op jit(solution)/shard_map/pallas_call | solution.py:56
  45.5 0.0 copy-start.3
  45.5 0.2 collective-permute-start.18
  45.7 2.8 %collective-permute-start.20 = (bf16[256,512]{1,0:T(8,128)(2,1)S(1)}, bf16[256,512]{1,0:T(8,128)(2,1)S(1)}, u32[]{:S(2)}, u32[]{:S(2)}) collective-permute-start(bf16[256,512]{1,0:T(8,128)(2,1)S(1)} %get-tuple-element.30.refs_0_), channel_id=1, source_target_pairs={{0,16},{1,17},{2,18},{3,19},{4,20},{5,21},{6,22},{7,23},{8,24},{9,... | collective-permute-start | bytes 786440 | tf_op jit(solution)/shard_map/ppermute | solution.py:26
  48.5 2.5 %collective-permute-start.19 = (bf16[256,512]{1,0:T(8,128)(2,1)S(1)}, bf16[256,512]{1,0:T(8,128)(2,1)S(1)}, u32[]{:S(2)}, u32[]{:S(2)}) collective-permute-start(bf16[256,512]{1,0:T(8,128)(2,1)S(1)} %get-tuple-element.30.refs_0_), channel_id=1, source_target_pairs={{0,8},{1,9},{2,10},{3,11},{4,12},{5,13},{6,14},{7,15},{8,0},{9,1},... | collective-permute-start | bytes 786440 | tf_op jit(solution)/shard_map/ppermute | solution.py:26
  51.0 4.9 %collective-permute-done.5.refs_2_ = bf16[1024,512]{1,0:T(8,128)(2,1)S(1)} collective-permute-done((bf16[1024,512]{1,0:T(8,128)(2,1)S(1)}, bf16[1024,512]{1,0:T(8,128)(2,1)S(1)}, u32[]{:S(2)}, u32[]{:S(2)}) %collective-permute-start.5) | collective-permute-done | bytes 1048608 | tf_op jit(solution)/shard_map/ppermute | solution.py:26
  55.9 1.5 %collective-permute-start.12 = (bf16[1024,512]{1,0:T(8,128)(2,1)S(1)}, bf16[1024,512]{1,0:T(8,128)(2,1)S(1)}, u32[]{:S(2)}, u32[]{:S(2)}) collective-permute-start(bf16[1024,512]{1,0:T(8,128)(2,1)S(1)} %collective-permute-done.refs_1_), channel_id=1, source_target_pairs={{0,2},{1,3},{2,0},{3,1},{4,5},{5,4},{6,7},{7,6},{8,10},{9,11},{10,... | collective-permute-start | bytes 3145736 | tf_op jit(solution)/shard_map/ppermute | solution.py:26
  57.5 3.6 %collective-permute-done.20.refs_2_ = bf16[256,512]{1,0:T(8,128)(2,1)S(1)} collective-permute-done((bf16[256,512]{1,0:T(8,128)(2,1)S(1)}, bf16[256,512]{1,0:T(8,128)(2,1)S(1)}, u32[]{:S(2)}, u32[]{:S(2)}) %collective-permute-start.20) | collective-permute-done | bytes 262176 | tf_op jit(solution)/shard_map/ppermute | solution.py:26
  61.1 0.1 collective-permute-done.19.refs_1_
  61.2 0.0 collective-permute-done.18.refs_5_.first_theirs
  61.2 1.6 %collective-permute-start.21 = (bf16[256,512]{1,0:T(8,128)(2,1)S(1)}, bf16[256,512]{1,0:T(8,128)(2,1)S(1)}, u32[]{:S(2)}, u32[]{:S(2)}) collective-permute-start(bf16[256,512]{1,0:T(8,128)(2,1)S(1)} %collective-permute-done.20.refs_2_), channel_id=1, source_target_pairs={{0,8},{1,9},{2,10},{3,11},{4,12},{5,13},{6,14},{7,15},{8,0},{9,1},... | collective-permute-start | bytes 786440 | tf_op jit(solution)/shard_map/ppermute | solution.py:26
  62.8 6.2 %collective-permute-done.21.refs_3_ = bf16[256,512]{1,0:T(8,128)(2,1)S(1)} collective-permute-done((bf16[256,512]{1,0:T(8,128)(2,1)S(1)}, bf16[256,512]{1,0:T(8,128)(2,1)S(1)}, u32[]{:S(2)}, u32[]{:S(2)}) %collective-permute-start.21) | collective-permute-done | bytes 262176 | tf_op jit(solution)/shard_map/ppermute | solution.py:26
  69.0 1.5 %shard_map.72.refs_4_ = bf16[1024,512]{1,0:T(8,128)(2,1)S(1)} custom-call(s32[3]{0:T(128)S(1)} %pad_add_fusion.place_ref, bf16[2,1024,1024]{2,1,0:T(8,128)(2,1)S(1)} %shard_map.69.inverse, bf16[256,512]{1,0:T(8,128)(2,1)S(1)} %get-tuple-element.30.refs_0_, bf16[256,512]{1,0:T(8,128)(2,1)S(1)} %collective-permute-done.19.refs_1_, ...), custom_call_target="tpu_custom_call" | custom-call | tf_op jit(solution)/shard_map/pallas_call | solution.py:56
  70.5 0.1 collective-permute-start.22
  70.6 0.1 collective-permute-done.12.refs_3_
  70.7 0.0 copy-done.3
  70.7 2.9 %shard_map.71.total = f32[1024,1024]{1,0:T(8,128)S(1)} custom-call(s32[3]{0:T(128)S(1)} %pad_add_fusion.place_ref, bf16[1024,1024]{1,0:T(8,128)(2,1)S(1)} %copy-done.3, bf16[1024,512]{1,0:T(8,128)(2,1)S(1)} %copy-done.1, bf16[1024,512]{1,0:T(8,128)(2,1)S(1)} %collective-permute-done.refs_1_, bf16[1024,512]{1,0:T(8,128)(2,1)S(1)} %collective-permute-done.5.refs_2_, ...), custom_call_target="tpu_custom_call" | custom-call | flops 4000000000 | tf_op jit(solution)/shard_map/pallas_call | solution.py:56
  73.7 0.0 collective-permute-done.22.refs_5_
  73.7 3.8 %shard_map.73 = (bf16[1024,1024]{1,0:T(8,128)(2,1)}, bf16[2,128,1024]{2,1,0:T(8,128)(2,1)}) custom-call(s32[3]{0:T(128)S(1)} %pad_add_fusion.place_ref, f32[1024,1024]{1,0:T(8,128)S(1)} %shard_map.71.total, bf16[1024,512]{1,0:T(8,128)(2,1)S(1)} %get-tuple-element.29.refs_4_.first, bf16[1024,512]{1,0:T(8,128)(2,1)S(1)} %collective-permute-done.18.refs_5_.first_theirs, ...), custom_call_target="tpu_custom_call" | custom-call | tf_op jit(solution)/shard_map/pallas_call | solution.py:56
  (5 shorter events, 0.1 us)
Async XLA Ops:
  0.6 1.0 %copy-start = (bf16[2,128,1024]{2,1,0:T(8,128)(2,1)S(1)}, bf16[2,128,1024]{2,1,0:T(8,128)(2,1)}, u32[]{:S(2)}) copy-start(bf16[2,128,1024]{2,1,0:T(8,128)(2,1)} %param.6) | copy-start | bytes 1572868
  2.8 12.9 %collective-permute-start.1 = (bf16[2,128,512]{2,1,0:T(8,128)(2,1)S(1)}, bf16[2,128,512]{2,1,0:T(8,128)(2,1)S(1)}, u32[]{:S(2)}, u32[]{:S(2)}) collective-permute-start(bf16[2,128,512]{2,1,0:T(8,128)(2,1)S(1)} %get-tuple-element.37), channel_id=1, source_target_pairs={{0,4},{1,5},{2,6},{3,7},{4,0},{5,1},{6,2},{7,3},{8,12},{9,13},{10,... | collective-permute-start | bytes 786440 | tf_op jit(solution)/shard_map/ppermute | solution.py:26
  3.3 9.3 %collective-permute-start.6 = (bf16[64,1024]{1,0:T(8,128)(2,1)S(1)}, bf16[64,1024]{1,0:T(8,128)(2,1)S(1)}, u32[]{:S(2)}, u32[]{:S(2)}) collective-permute-start(bf16[64,1024]{1,0:T(8,128)(2,1)S(1)} %bitcast.12), channel_id=1, source_target_pairs={{0,8},{1,9},{2,10},{3,11},{4,12},{5,13},{6,14},{7,15},{8,0},{9,1},... | collective-permute-start | bytes 393224 | tf_op jit(solution)/shard_map/ppermute | solution.py:26
  5.9 9.3 %collective-permute-start.2 = (bf16[64,1024]{1,0:T(8,128)(2,1)S(1)}, bf16[64,1024]{1,0:T(8,128)(2,1)S(1)}, u32[]{:S(2)}, u32[]{:S(2)}) collective-permute-start(bf16[64,1024]{1,0:T(8,128)(2,1)S(1)} %bitcast.13), channel_id=1, source_target_pairs={{0,16},{1,17},{2,18},{3,19},{4,20},{5,21},{6,22},{7,23},{8,24},{9,... | collective-permute-start | bytes 393224 | tf_op jit(solution)/shard_map/ppermute | solution.py:26
  8.5 31.9 %collective-permute-start = (bf16[1024,512]{1,0:T(8,128)(2,1)}, bf16[1024,512]{1,0:T(8,128)(2,1)S(1)}, u32[]{:S(2)}, u32[]{:S(2)}) collective-permute-start(bf16[1024,512]{1,0:T(8,128)(2,1)} %refs_0_.3), channel_id=1, source_target_pairs={{0,1},{1,0},{2,3},{3,2},{4,6},{5,7},{6,4},{7,5},{8,9},{9,8},{10,11... | collective-permute-start | bytes 3145736 | tf_op jit(solution)/shard_map/ppermute | solution.py:26
  15.3 6.9 %collective-permute-start.7 = (bf16[64,1024]{1,0:T(8,128)(2,1)S(1)}, bf16[64,1024]{1,0:T(8,128)(2,1)S(1)}, u32[]{:S(2)}, u32[]{:S(2)}) collective-permute-start(bf16[64,1024]{1,0:T(8,128)(2,1)S(1)} %collective-permute-done.2.refs_2_), channel_id=1, source_target_pairs={{0,8},{1,9},{2,10},{3,11},{4,12},{5,13},{6,14},{7,15},{8,0},{9,1},... | collective-permute-start | bytes 393224 | tf_op jit(solution)/shard_map/ppermute | solution.py:26
  15.8 14.2 %copy-start.2 = (bf16[128,1024]{1,0:T(8,128)(2,1)S(1)}, bf16[128,1024]{1,0:T(8,128)(2,1)}, u32[]{:S(2)}) copy-start(bf16[128,1024]{1,0:T(8,128)(2,1)} %mine.1) | copy-start | bytes 786436
  15.8 25.4 %copy-start.1 = (bf16[1024,512]{1,0:T(8,128)(2,1)S(1)}, bf16[1024,512]{1,0:T(8,128)(2,1)}, u32[]{:S(2)}) copy-start(bf16[1024,512]{1,0:T(8,128)(2,1)} %refs_0_.3) | copy-start | bytes 3145732
  15.8 14.1 %collective-permute-start.3 = (bf16[256,512]{1,0:T(8,128)(2,1)S(1)}, bf16[256,512]{1,0:T(8,128)(2,1)S(1)}, u32[]{:S(2)}, u32[]{:S(2)}) collective-permute-start(bf16[256,512]{1,0:T(8,128)(2,1)S(1)} %slice_bitcast_fusion.1), channel_id=1, source_target_pairs={{0,16},{1,17},{2,18},{3,19},{4,20},{5,21},{6,22},{7,23},{8,24},{9,... | collective-permute-start | bytes 786440 | tf_op jit(solution)/shard_map/ppermute | solution.py:26
  22.8 9.9 %collective-permute-start.9 = (bf16[32,5120]{1,0:T(8,128)(2,1)S(1)}, bf16[32,5120]{1,0:T(8,128)(2,1)S(1)}, u32[]{:S(2)}, u32[]{:S(2)}) collective-permute-start(bf16[32,5120]{1,0:T(8,128)(2,1)S(1)} %shard_map.68.refs_0_), channel_id=1, source_target_pairs={{0,2},{1,3},{2,0},{3,1},{4,5},{5,4},{6,7},{7,6},{8,10},{9,11},{10,... | collective-permute-start | bytes 983048 | tf_op jit(solution)/shard_map/ppermute | solution.py:26
  24.4 8.3 %collective-permute-start.8 = (bf16[32,5120]{1,0:T(8,128)(2,1)S(1)}, bf16[32,5120]{1,0:T(8,128)(2,1)S(1)}, u32[]{:S(2)}, u32[]{:S(2)}) collective-permute-start(bf16[32,5120]{1,0:T(8,128)(2,1)S(1)} %shard_map.68.refs_0_), channel_id=1, source_target_pairs={{0,1},{1,0},{2,3},{3,2},{4,6},{5,7},{6,4},{7,5},{8,9},{9,8},{10,11... | collective-permute-start | bytes 983048 | tf_op jit(solution)/shard_map/ppermute | solution.py:26
  26.2 6.5 %collective-permute-start.10 = (bf16[256,512]{1,0:T(8,128)(2,1)S(1)}, bf16[256,512]{1,0:T(8,128)(2,1)S(1)}, u32[]{:S(2)}, u32[]{:S(2)}) collective-permute-start(bf16[256,512]{1,0:T(8,128)(2,1)S(1)} %slice_bitcast_fusion), channel_id=1, source_target_pairs={{0,8},{1,9},{2,10},{3,11},{4,12},{5,13},{6,14},{7,15},{8,0},{9,1},... | collective-permute-start | bytes 786440 | tf_op jit(solution)/shard_map/ppermute | solution.py:26
  29.9 2.8 %collective-permute-start.4 = (bf16[128,1024]{1,0:T(8,128)(2,1)S(1)}, bf16[128,1024]{1,0:T(8,128)(2,1)S(1)}, u32[]{:S(2)}, u32[]{:S(2)}) collective-permute-start(bf16[128,1024]{1,0:T(8,128)(2,1)S(1)} %copy-done.2), channel_id=1, source_target_pairs={{0,4},{1,5},{2,6},{3,7},{4,0},{5,1},{6,2},{7,3},{8,12},{9,13},{10,... | collective-permute-start | bytes 786440 | tf_op jit(solution)/shard_map/ppermute | solution.py:26
  32.7 7.1 %collective-permute-start.11 = (bf16[32,5120]{1,0:T(8,128)(2,1)S(1)}, bf16[32,5120]{1,0:T(8,128)(2,1)S(1)}, u32[]{:S(2)}, u32[]{:S(2)}) collective-permute-start(bf16[32,5120]{1,0:T(8,128)(2,1)S(1)} %collective-permute-done.8.refs_1_), channel_id=1, source_target_pairs={{0,2},{1,3},{2,0},{3,1},{4,5},{5,4},{6,7},{7,6},{8,10},{9,11},{10,... | collective-permute-start | bytes 983048 | tf_op jit(solution)/shard_map/ppermute | solution.py:26
  34.3 6.8 %collective-permute-start.17 = (bf16[256,512]{1,0:T(8,128)(2,1)S(1)}, bf16[256,512]{1,0:T(8,128)(2,1)S(1)}, u32[]{:S(2)}, u32[]{:S(2)}) collective-permute-start(bf16[256,512]{1,0:T(8,128)(2,1)S(1)} %collective-permute-done.3.refs_2_), channel_id=1, source_target_pairs={{0,8},{1,9},{2,10},{3,11},{4,12},{5,13},{6,14},{7,15},{8,0},{9,1},... | collective-permute-start | bytes 786440 | tf_op jit(solution)/shard_map/ppermute | solution.py:26
  39.9 2.8 %collective-permute-start.16 = (bf16[32,5120]{1,0:T(8,128)(2,1)S(1)}, bf16[32,5120]{1,0:T(8,128)(2,1)S(1)}, u32[]{:S(2)}, u32[]{:S(2)}) collective-permute-start(bf16[32,5120]{1,0:T(8,128)(2,1)S(1)} %collective-permute-done.11.refs_3_), channel_id=1, source_target_pairs={{0,4},{1,5},{2,6},{3,7},{4,0},{5,1},{6,2},{7,3},{8,12},{9,13},{10,... | collective-permute-start | bytes 983048 | tf_op jit(solution)/shard_map/ppermute | solution.py:26
  39.9 2.8 %collective-permute-start.13 = (bf16[32,5120]{1,0:T(8,128)(2,1)S(1)}, bf16[32,5120]{1,0:T(8,128)(2,1)S(1)}, u32[]{:S(2)}, u32[]{:S(2)}) collective-permute-start(bf16[32,5120]{1,0:T(8,128)(2,1)S(1)} %shard_map.68.refs_0_), channel_id=1, source_target_pairs={{0,4},{1,5},{2,6},{3,7},{4,0},{5,1},{6,2},{7,3},{8,12},{9,13},{10,... | collective-permute-start | bytes 983048 | tf_op jit(solution)/shard_map/ppermute | solution.py:26
  40.4 2.3 %collective-permute-start.15 = (bf16[32,5120]{1,0:T(8,128)(2,1)S(1)}, bf16[32,5120]{1,0:T(8,128)(2,1)S(1)}, u32[]{:S(2)}, u32[]{:S(2)}) collective-permute-start(bf16[32,5120]{1,0:T(8,128)(2,1)S(1)} %collective-permute-done.9.refs_2_), channel_id=1, source_target_pairs={{0,4},{1,5},{2,6},{3,7},{4,0},{5,1},{6,2},{7,3},{8,12},{9,13},{10,... | collective-permute-start | bytes 983048 | tf_op jit(solution)/shard_map/ppermute | solution.py:26
  40.4 2.5 %collective-permute-start.14 = (bf16[32,5120]{1,0:T(8,128)(2,1)S(1)}, bf16[32,5120]{1,0:T(8,128)(2,1)S(1)}, u32[]{:S(2)}, u32[]{:S(2)}) collective-permute-start(bf16[32,5120]{1,0:T(8,128)(2,1)S(1)} %collective-permute-done.8.refs_1_), channel_id=1, source_target_pairs={{0,4},{1,5},{2,6},{3,7},{4,0},{5,1},{6,2},{7,3},{8,12},{9,13},{10,... | collective-permute-start | bytes 983048 | tf_op jit(solution)/shard_map/ppermute | solution.py:26
  41.1 14.8 %collective-permute-start.5 = (bf16[1024,512]{1,0:T(8,128)(2,1)S(1)}, bf16[1024,512]{1,0:T(8,128)(2,1)S(1)}, u32[]{:S(2)}, u32[]{:S(2)}) collective-permute-start(bf16[1024,512]{1,0:T(8,128)(2,1)S(1)} %copy-done.1), channel_id=1, source_target_pairs={{0,2},{1,3},{2,0},{3,1},{4,5},{5,4},{6,7},{7,6},{8,10},{9,11},{10,... | collective-permute-start | bytes 3145736 | tf_op jit(solution)/shard_map/ppermute | solution.py:26
  45.5 25.3 %copy-start.3 = (bf16[1024,1024]{1,0:T(8,128)(2,1)S(1)}, bf16[1024,1024]{1,0:T(8,128)(2,1)}, u32[]{:S(2)}) copy-start(bf16[1024,1024]{1,0:T(8,128)(2,1)} %rhs.1) | copy-start | bytes 6291460
  45.5 15.7 %collective-permute-start.18 = (bf16[1024,512]{1,0:T(8,128)(2,1)S(1)}, bf16[1024,512]{1,0:T(8,128)(2,1)S(1)}, u32[]{:S(2)}, u32[]{:S(2)}) collective-permute-start(bf16[1024,512]{1,0:T(8,128)(2,1)S(1)} %get-tuple-element.29.refs_4_.first), channel_id=1, source_target_pairs={{0,4},{1,5},{2,6},{3,7},{4,0},{5,1},{6,2},{7,3},{8,12},{9,13},{10,... | collective-permute-start | bytes 3145736 | tf_op jit(solution)/shard_map/ppermute | solution.py:26
  45.7 15.4 %collective-permute-start.20 = (bf16[256,512]{1,0:T(8,128)(2,1)S(1)}, bf16[256,512]{1,0:T(8,128)(2,1)S(1)}, u32[]{:S(2)}, u32[]{:S(2)}) collective-permute-start(bf16[256,512]{1,0:T(8,128)(2,1)S(1)} %get-tuple-element.30.refs_0_), channel_id=1, source_target_pairs={{0,16},{1,17},{2,18},{3,19},{4,20},{5,21},{6,22},{7,23},{8,24},{9,... | collective-permute-start | bytes 786440 | tf_op jit(solution)/shard_map/ppermute | solution.py:26
  48.5 12.6 %collective-permute-start.19 = (bf16[256,512]{1,0:T(8,128)(2,1)S(1)}, bf16[256,512]{1,0:T(8,128)(2,1)S(1)}, u32[]{:S(2)}, u32[]{:S(2)}) collective-permute-start(bf16[256,512]{1,0:T(8,128)(2,1)S(1)} %get-tuple-element.30.refs_0_), channel_id=1, source_target_pairs={{0,8},{1,9},{2,10},{3,11},{4,12},{5,13},{6,14},{7,15},{8,0},{9,1},... | collective-permute-start | bytes 786440 | tf_op jit(solution)/shard_map/ppermute | solution.py:26
  55.9 14.8 %collective-permute-start.12 = (bf16[1024,512]{1,0:T(8,128)(2,1)S(1)}, bf16[1024,512]{1,0:T(8,128)(2,1)S(1)}, u32[]{:S(2)}, u32[]{:S(2)}) collective-permute-start(bf16[1024,512]{1,0:T(8,128)(2,1)S(1)} %collective-permute-done.refs_1_), channel_id=1, source_target_pairs={{0,2},{1,3},{2,0},{3,1},{4,5},{5,4},{6,7},{7,6},{8,10},{9,11},{10,... | collective-permute-start | bytes 3145736 | tf_op jit(solution)/shard_map/ppermute | solution.py:26
  61.2 7.9 %collective-permute-start.21 = (bf16[256,512]{1,0:T(8,128)(2,1)S(1)}, bf16[256,512]{1,0:T(8,128)(2,1)S(1)}, u32[]{:S(2)}, u32[]{:S(2)}) collective-permute-start(bf16[256,512]{1,0:T(8,128)(2,1)S(1)} %collective-permute-done.20.refs_2_), channel_id=1, source_target_pairs={{0,8},{1,9},{2,10},{3,11},{4,12},{5,13},{6,14},{7,15},{8,0},{9,1},... | collective-permute-start | bytes 786440 | tf_op jit(solution)/shard_map/ppermute | solution.py:26
  70.5 3.2 %collective-permute-start.22 = (bf16[1024,512]{1,0:T(8,128)(2,1)S(1)}, bf16[1024,512]{1,0:T(8,128)(2,1)S(1)}, u32[]{:S(2)}, u32[]{:S(2)}) collective-permute-start(bf16[1024,512]{1,0:T(8,128)(2,1)S(1)} %shard_map.72.refs_4_), channel_id=1, source_target_pairs={{0,4},{1,5},{2,6},{3,7},{4,0},{5,1},{6,2},{7,3},{8,12},{9,13},{10,... | collective-permute-start | bytes 3145736 | tf_op jit(solution)/shard_map/ppermute | solution.py:26
